TPU v7x, 512 devices: a whole 4x4x16 slice. The times are simulated.
512 devices in a mesh: src: 16 (over z_lo, core), rcv: 32 (over y, x, z_hi).
Axes of the slice: x: 4, y: 4, z: 16 (z_hi: 2, z_lo: 8; z = z_hi * 8 + z_lo), core: 2. Of those that a mesh axis runs over, the one named last changes fastest.
Arguments:
- spectra: bfloat16 [768, 2, 2, 10240], P('rcv', None, None, 'src'), may hold values from -4000 to 4000
Outputs:
- cross: float32 [10240, 2, 2, 10240], P('src', None, None, 'rcv')
All inputs are finite; a program needn't handle non-finite values.
Results may differ from a plain program's by a relative error of at most 0.0037.
Values may be sent and summed in bfloat16 or wider, within the bound.
No kernel may reach another device: no remote copies, remote signals or barrier semaphores. Data moves between devices by JAX's collectives and lax.ppermute only.
A program may use at most 64 MiB of HBM per device.

v0:
```python
import math

import jax
import jax.numpy as jnp
from jax import lax
from jax.sharding import PartitionSpec as P

water_factor = 0.5
tiny_eps = 1e-06


def from_root(block, axis, owner):
    block = jnp.where(lax.axis_index(axis) == owner, block, jnp.zeros_like(block))
    return lax.psum(block, axis)


def whiten_with(values, water_level):
    energy = values[:, 0] ** 2 + values[:, 1] ** 2
    denom = jnp.sqrt(energy + water_factor * water_level[None] + tiny_eps)
    return (values / denom[:, None]).astype(jnp.bfloat16)


def on_device(spectra):
    group_size = lax.axis_size("rcv") // lax.axis_size("src")
    half_width = spectra.shape[3] // group_size
    values = spectra.astype(jnp.float32)
    energy = values[:, 0] ** 2 + values[:, 1] ** 2
    power_total = lax.psum(jnp.sum(energy, axis=0), "rcv")
    water_level = power_total / (spectra.shape[0] * lax.axis_size("rcv"))
    gathered = lax.all_gather(whiten_with(values, water_level), "rcv", axis=0, tiled=True)
    column = lax.axis_index("rcv")
    owner_row = column // group_size
    offset = column % group_size * half_width
    received = from_root(gathered, "src", owner_row)
    receiver = lax.dynamic_slice_in_dim(received, offset, half_width, 3)
    flipped = jnp.stack([gathered[:, 1], -gathered[:, 0]], axis=1)
    real_part = jnp.einsum("wpfc,wpfd->cfd", gathered, receiver, preferred_element_type=jnp.float32)
    imag_part = jnp.einsum("wpfc,wpfd->cfd", flipped, receiver, preferred_element_type=jnp.float32)
    stack_scale = jnp.float32(1.0 / math.sqrt(gathered.shape[0]))
    return jnp.stack([real_part, imag_part], axis=1) * stack_scale


def solution(mesh):
    return jax.shard_map(
        on_device,
        mesh=mesh,
        in_specs=(P("rcv", None, None, "src"),),
        out_specs=P("src", None, None, "rcv"),
        check_vma=False,
    )
```

profile of v0, /device:TPU:1, one launch (start us, length us, event | category | flops | bytes accessed | tf_op | source)
XLA Modules:
  0.0 557.2 jit_solution(4480337713861895139)
XLA Ops:
  6.5 0.0 all-gather.2.cloned.1.call-start
  6.5 0.9 copy_convert_fusion
  7.5 153.6 %psum.14 = f32[2,640]{1,0:T(2,128)S(1)} all-reduce(f32[2,640]{1,0:T(2,128)S(1)} %fusion.16), channel_id=1, replica_groups=mesh['src'=16,'rcv'=32] {'rcv'}, use_global_device_ids=true, to_apply=%region_1.0 | all-reduce | flops 1280 | bytes 10240 | tf_op jit(solution)/shard_map/psum | solution.py:28
  161.1 0.1 sqrt_bitcast_fusion
  161.1 1.6 divide_convert_fusion
  162.7 0.0 all-gather.2.cloned.1.call-update
  162.7 0.0 all-reduce.2.cloned.1.call-start
  162.8 161.9 %all-gather.2.cloned.1.call-done = bf16[768,2,2,640]{3,0,1,2:T(8,128)(2,1)} async-done(((bf16[24,2,2,640]{3,0,1,2:T(8,128)(2,1)}), bf16[768,2,2,640]{3,0,1,2:T(8,128)(2,1)}) %all-gather.2.cloned.1.call-update) | async-done | bytes 3932176 | tf_op jit(solution)/shard_map/all_gather | solution.py:30
  324.7 2.3 broadcast_select_fusion
  327.0 0.0 all-reduce.2.cloned.1.call-update
  327.0 3.7 fusion.20
  330.8 208.8 %all-reduce.2.cloned.1.call-done = bf16[768,2,2,640]{3,0,1,2:T(8,128)(2,1)} async-done(((bf16[768,2,2,640]{3,0,1,2:T(8,128)(2,1)}), bf16[768,2,2,640]{3,0,1,2:T(8,128)(2,1)}) %all-reduce.2.cloned.1.call-update) | async-done | bytes 3932176 | tf_op jit(solution)/shard_map/psum | solution.py:14
  539.5 0.0 copy-start
  539.5 0.0 copy-start.1
  539.5 5.9 %fusion.12 = f32[640,1,2,320]{0,3,2,1:T(8,128)S(1)} fusion(bf16[768,2,2,640]{3,0,1,2:T(8,128)(2,1)} %all-gather.2.cloned.1.call-done, bf16[768,2,2,640]{3,0,1,2:T(8,128)(2,1)} %all-reduce.2.cloned.1.call-done, s32[]{:T(128)S(6)} %select_n.26), kind=kOutput, calls=%fused_computation.11 | convolution fusion | flops 1258291200 | bytes 7929860 | tf_op jit(solution)/shard_map/wpfc,wpfd->cfd/dot_general | solution.py:37
  545.5 0.0 copy-done
  545.5 0.0 copy-done.1
  545.5 2.9 fusion.7
  548.4 2.0 maximum_multiply_fusion
  (2 shorter events, 0.0 us)
Async XLA Ops:
  6.5 318.1 %all-gather.2.cloned.1.call-start = ((), (), s32[]{:S(2)}) async-start(), calls=%async_computation | async-start | bytes 4055040 | tf_op jit(solution)/shard_map/all_gather | solution.py:30
  162.7 376.8 %all-reduce.2.cloned.1.call-start = ((), (), s32[]{:S(2)}) async-start(), calls=%async_computation.1 | async-start | bytes 7864320 | tf_op jit(solution)/shard_map/psum | solution.py:14
  539.5 6.0 %copy-start = (bf16[768,1,2,640]{3,0,1,2:T(8,128)(2,1)S(1)}, bf16[768,1,2,640]{3,0,1,2:T(8,128)(2,1)}, u32[]{:S(2)}) copy-start(bf16[768,1,2,640]{3,0,1,2:T(8,128)(2,1)} %get-tuple-element.6) | copy-start | bytes 5898244
  539.5 6.0 %copy-start.1 = (bf16[768,2,2,640]{3,0,1,2:T(8,128)(2,1)S(1)}, bf16[768,2,2,640]{3,0,1,2:T(8,128)(2,1)}, u32[]{:S(2)}) copy-start(bf16[768,2,2,640]{3,0,1,2:T(8,128)(2,1)} %all-reduce.2.cloned.1.call-done) | copy-start | bytes 11796484
Sparse Core Ops, SparseCore 0:
  162.9 161.7 all-gather.1
  327.6 211.8 all-reduce.1
where the time goes:
time: 559 us; the launch traced here: 557 us
  waiting for transfers between devices  371 us (66%)
  blocking collectives  154 us (28%)
  between operations  13.5 us (2%)
  other arithmetic  10.7 us (2%)
  matrix products  8.81 us (2%)
    psum x1, waiting for transfers between devices, from_root(): return lax.psum(block, axis)  209 us
    all_gather x1, waiting for transfers between devices, on_device(): lax.all_gather(whiten_with(values, water_level), 'rcv', axis=0, tiled=True)  162 us
    psum x1, blocking collectives, on_device(): power_total = lax.psum(jnp.sum(energy, axis=0), 'rcv')  154 us
  transfers between devices with their start and end apart: 2, of which 2 were waited for; matrix products, arithmetic and copies ran while one was open for 1% of the time, Pallas kernels for 0%

commit v1 on v0

v1 whole, which is shorter than its diff:
```python
import functools
import math

import jax
import jax.numpy as jnp
from jax import lax
from jax.experimental import pallas as pl
from jax.experimental.pallas import tpu as pltpu
from jax.sharding import Mesh, PartitionSpec as P

water_factor = 0.5
tiny_eps = 1e-06

SIZES = dict(zl=8, core=2, y=4, x=4, zh=2)
AXES = tuple(SIZES)


def coordinates():
    out = [()]
    for size in SIZES.values():
        out = [c + (i,) for c in out for i in range(size)]
    return out


def number(c):
    n = 0
    for i, size in zip(c, SIZES.values()):
        n = n * size + i % size
    return n


def permute(value, target):
    pairs = [(number(c), number(target(*c))) for c in coordinates()]
    return lax.ppermute(value, AXES, pairs)


def fetch_first(value, offset):
    def target(zl, core, y, x, zh):
        return (zl, core, y, x - offset, zh) if core == 0 else (zl, core, y - offset, x, zh)

    return permute(value, target)


def fetch_second(value, offset):
    def target(zl, core, y, x, zh):
        return (zl, core, y - offset, x, zh) if core == 0 else (zl, core, y, x - offset, zh)

    return permute(value, target)


def gather_plane(block):
    first = jnp.stack([block] + [fetch_first(block, o) for o in (1, 2, 3)])
    return [first] + [fetch_second(first, o) for o in (1, 2, 3)]


def to_column(value, cross):
    def target(zl, core, y, x, zh):
        s, g = zl * 2 + core, y * 4 + x
        return (g // 2, g % 2, s // 4, s % 4, 1 - zh if cross else zh)

    return permute(value, target)


def along_column(value, distance):
    return permute(value, lambda zl, core, y, x, zh: (zl ^ distance, core, y, x, zh))


def spectra_kernel(place, *refs):
    sources, receivers, out, wide, left, left_turned = refs[:8], refs[8:10], refs[10], refs[11], refs[12], refs[13]
    zl, core, y, x = place[0], place[1], place[2], place[3]
    rows = sources[0].shape[2]
    half = rows // 2
    channels = sources[0].shape[3]
    width = channels // 2
    windows = 32 * half

    def energy_of(block):
        values = block.astype(jnp.float32)
        real, imag = values[:half], values[half:]
        return real, imag, real * real + imag * imag

    def fold(energy):
        return energy.reshape(half // 8, 8, channels).sum(axis=0)

    def level(total):
        return (water_factor / windows) * jnp.sum(total, axis=0, keepdims=True) + tiny_eps

    zero = jnp.zeros((8, channels), jnp.float32)
    for f in range(2):
        total = zero
        for ref in sources:
            total = lax.fori_loop(0, 4, lambda a, t, ref=ref: t + fold(energy_of(ref[a, f])[2]), total)
        floor = level(total)
        for n, ref in enumerate(sources):
            zr, second = n // 4, n % 4

            def body(a, carry, ref=ref, zr=zr, second=second):
                real, imag, energy = energy_of(ref[a, f])
                scale = lax.rsqrt(energy + floor)
                gy = lax.rem(y + jnp.where(core == 0, second, a), 4)
                gx = lax.rem(x + jnp.where(core == 0, a, second), 4)
                row = pl.multiple_of((zr * 16 + gy * 4 + gx) * rows, rows)
                block = jnp.concatenate([real * scale, imag * scale], axis=0).astype(jnp.bfloat16)
                wide[f, pl.ds(row, rows), :] = block
                return carry

            lax.fori_loop(0, 4, body, 0)

    total = zero
    for ref in receivers:
        total = lax.fori_loop(
            0, 8, lambda a, t, ref=ref: t + fold(energy_of(ref[a, 0])[2]) + fold(energy_of(ref[a, 1])[2]), total
        )
    floor = level(total)
    for n, ref in enumerate(receivers):

        def body(a, carry, ref=ref, n=n):
            other = lax.bitwise_xor(zl, (a % 2) * 4 + (a // 2 % 2) * 2 + a // 4)
            g = other * 2 + lax.bitwise_xor(core, n)
            for zr in range(2):
                real, imag, energy = energy_of(ref[a, zr])
                scale = lax.rsqrt(energy + floor)
                real, imag = real * scale, imag * scale
                row = pl.multiple_of((zr * 16 + g) * rows, rows)
                block = jnp.concatenate([real, imag], axis=0).astype(jnp.bfloat16)
                turned = jnp.concatenate([-imag, real], axis=0).astype(jnp.bfloat16)
                for f in range(2):
                    left[f, pl.ds(row, rows), :] = block[:, f * width : (f + 1) * width]
                    left_turned[f, pl.ds(row, rows), :] = turned[:, f * width : (f + 1) * width]
            return carry

        lax.fori_loop(0, 8, body, 0)

    stack_scale = 1.0 / math.sqrt(windows)
    for f in range(2):
        for part, ref in enumerate((left, left_turned)):
            product = lax.dot_general(
                ref[f], wide[f], (((0,), (0,)), ((), ())), preferred_element_type=jnp.float32
            )
            out[part, f] = product * stack_scale


def cross_spectra(place, sources, receivers):
    depth = 32 * sources[0].shape[2]
    channels = sources[0].shape[3]
    vmem = pl.BlockSpec(memory_space=pltpu.VMEM)
    return pl.pallas_call(
        spectra_kernel,
        out_shape=jax.ShapeDtypeStruct((2, 2, channels // 2, channels), jnp.float32),
        in_specs=[pl.BlockSpec(memory_space=pltpu.SMEM)] + [vmem] * 10,
        out_specs=vmem,
        scratch_shapes=[
            pltpu.VMEM((2, depth, channels), jnp.bfloat16),
            pltpu.VMEM((2, depth, channels // 2), jnp.bfloat16),
            pltpu.VMEM((2, depth, channels // 2), jnp.bfloat16),
        ],
        compiler_params=pltpu.CompilerParams(vmem_limit_bytes=48 * 1024 * 1024),
    )(place, *sources, *receivers)


def on_device(spectra):
    windows, _, freqs, channels = spectra.shape
    width = channels // 2
    place = jnp.stack([lax.axis_index(a) for a in ("zl", "core", "y", "x")]).astype(jnp.int32)
    zh = lax.axis_index("zh")
    block = jnp.transpose(spectra, (2, 1, 0, 3)).reshape(freqs, 2 * windows, channels)

    low = jnp.concatenate([block[0, :, :width], block[1, :, :width]], axis=1)
    high = jnp.concatenate([block[0, :, width:], block[1, :, width:]], axis=1)
    mine = jnp.where(zh == 0, low, high)
    theirs = jnp.where(zh == 0, high, low)
    held = jnp.stack([to_column(mine, False), to_column(theirs, True)])[None]
    partner = permute(block, lambda zl, core, y, x, zh: (zl, core, y, x, 1 - zh))
    sources = gather_plane(block) + gather_plane(partner)

    for distance in (4, 2, 1):
        held = jnp.concatenate([held, along_column(held, distance)])
    other = permute(held, lambda zl, core, y, x, zh: (zl, 1 - core, y, x, zh))

    crossed = cross_spectra(place, sources, [held, other])
    return jnp.transpose(crossed, (3, 0, 1, 2))


def solution(mesh):
    fine = Mesh(mesh.devices.reshape(tuple(SIZES.values())), AXES)
    return jax.shard_map(
        on_device,
        mesh=fine,
        in_specs=(P(("y", "x", "zh"), None, None, ("zl", "core")),),
        out_specs=P(("zl", "core"), None, None, ("y", "x", "zh")),
        check_vma=False,
    )
```

time: 559 us -> 147 us (0.26)
  waiting for transfers between devices: 371 us -> 28.8 us
  blocking collectives: 154 us -> 0 us
  starting transfers between devices: 0.04 us -> 102 us
  between operations: 13.5 us -> 0.29 us
  Pallas kernels: 0 us -> 12 us
  other arithmetic: 10.7 us -> 0.56 us
  matrix products: 8.81 us -> 0 us
    psum x1 -> x0, waiting for transfers between devices: 209 us -> none  [from_root(): return lax.psum(block, axis)]
    all_gather x1 -> x0, waiting for transfers between devices: 162 us -> none  [on_device(): lax.all_gather(whiten_with(values, water_level), 'rcv', axis=0, tiled=True)]
    psum x1 -> x0, blocking collectives: 154 us -> none  [on_device(): power_total = lax.psum(jnp.sum(energy, axis=0), 'rcv')]
    ppermute x0 -> x19, starting transfers between devices: none -> 102 us  [permute(): return lax.ppermute(value, AXES, pairs)]
    ppermute x0 -> x19, waiting for transfers between devices: none -> 28.8 us  [permute(): return lax.ppermute(value, AXES, pairs)]
    pallas_call x0 -> x1, Pallas kernels: none -> 12 us  [cross_spectra(): pl.pallas_call(spectra_kernel, out_shape=jax.ShapeDtypeStruct((2, 2, chan...]
    dot_general x2 -> x0, matrix products: 8.81 us -> none  [the longest x1 5.95 us: on_device(): jnp.einsum('wpfc,wpfd->cfd', gathered, receiver, preferred_element_type=j...]
  transfers between devices with their start and end apart: 2 -> 19, of which waited for: 2 -> 7; matrix products, arithmetic and copies ran while one was open for 1% -> 0% of each run, Pallas kernels for 0% -> 0%
where the time goes in v1:
time: 147 us; the launch traced here: 146 us
  starting transfers between devices  102 us (69%)
  waiting for transfers between devices  28.8 us (20%)
  Pallas kernels  12 us (8%)
  local copies, waits for them, and re-layouts  2.81 us (2%)
    ppermute x19, starting transfers between devices, permute(): return lax.ppermute(value, AXES, pairs)  102 us
    ppermute x19, waiting for transfers between devices, permute(): return lax.ppermute(value, AXES, pairs)  28.8 us
    pallas_call x1, Pallas kernels, cross_spectra(): pl.pallas_call(spectra_kernel, out_shape=jax.ShapeDtypeStruct((2, 2, chan...  12 us
  transfers between devices with their start and end apart: 19, of which 7 were waited for; matrix products, arithmetic and copies ran while one was open for 0% of the time, Pallas kernels for 0%

profile of v1, /device:TPU:1, one launch (start us, length us, event | category | flops | bytes accessed | tf_op | source)
XLA Modules:
  0.0 146.3 jit_solution(14200788124068410666)
XLA Ops:
  0.0 0.9 copy.2
  0.9 0.1 slice_bitcast_fusion.3
  1.0 0.1 broadcast_select_fusion.1
  1.1 4.5 %collective-permute-start.13 = (bf16[48,640]{1,0:T(8,128)(2,1)S(1)}, bf16[48,640]{1,0:T(8,128)(2,1)S(1)}, u32[]{:S(2)}, u32[]{:S(2)}) collective-permute-start(bf16[48,640]{1,0:T(8,128)(2,1)S(1)} %get-tuple-element.5), channel_id=1, source_target_pairs={{0,0},{1,1},{2,32},{3,33},{4,64},{5,65},{6,96},{7,97},{8,128},{9,1... | collective-permute-start | bytes 184328 | tf_op jit(solution)/shard_map/ppermute | solution.py:34
  5.6 15.2 %collective-permute-start.14 = (bf16[48,640]{1,0:T(8,128)(2,1)S(1)}, bf16[48,640]{1,0:T(8,128)(2,1)S(1)}, u32[]{:S(2)}, u32[]{:S(2)}) collective-permute-start(bf16[48,640]{1,0:T(8,128)(2,1)S(1)} %get-tuple-element.6), channel_id=1, source_target_pairs={{0,1},{1,0},{2,33},{3,32},{4,65},{5,64},{6,97},{7,96},{8,129},{9,1... | collective-permute-start | bytes 184328 | tf_op jit(solution)/shard_map/ppermute | solution.py:34
  20.8 0.0 collective-permute-done.13
  20.8 1.9 %collective-permute-done.14 = bf16[48,640]{1,0:T(8,128)(2,1)S(1)} collective-permute-done((bf16[48,640]{1,0:T(8,128)(2,1)S(1)}, bf16[48,640]{1,0:T(8,128)(2,1)S(1)}, u32[]{:S(2)}, u32[]{:S(2)}) %collective-permute-start.14) | collective-permute-done | bytes 61472 | tf_op jit(solution)/shard_map/ppermute | solution.py:34
  22.8 11.0 %collective-permute-start.15 = (bf16[1,2,48,640]{3,2,1,0:T(8,128)(2,1)S(1)}, bf16[1,2,48,640]{3,2,1,0:T(8,128)(2,1)S(1)}, u32[]{:S(2)}, u32[]{:S(2)}) collective-permute-start(bf16[1,2,48,640]{3,2,1,0:T(8,128)(2,1)S(1)} %maximum_bitcast_fusion), channel_id=1, source_target_pairs={{0,256},{1,257},{2,258},{3,259},{4,260},{5,261},{6,262},{7,263},{8... | collective-permute-start | bytes 368648 | tf_op jit(solution)/shard_map/ppermute | solution.py:34
  33.7 3.2 %collective-permute-done.15 = bf16[1,2,48,640]{3,2,1,0:T(8,128)(2,1)S(1)} collective-permute-done((bf16[1,2,48,640]{3,2,1,0:T(8,128)(2,1)S(1)}, bf16[1,2,48,640]{3,2,1,0:T(8,128)(2,1)S(1)}, u32[]{:S(2)}, u32[]{:S(2)}) %collective-permute-start.15) | collective-permute-done | bytes 122912 | tf_op jit(solution)/shard_map/ppermute | solution.py:34
  37.0 8.8 %collective-permute-start.16 = (bf16[2,2,48,640]{3,2,1,0:T(8,128)(2,1)S(1)}, bf16[2,2,48,640]{3,2,1,0:T(8,128)(2,1)S(1)}, u32[]{:S(2)}, u32[]{:S(2)}) collective-permute-start(bf16[2,2,48,640]{3,2,1,0:T(8,128)(2,1)S(1)} %pad_maximum_fusion.4), channel_id=1, source_target_pairs={{0,128},{1,129},{2,130},{3,131},{4,132},{5,133},{6,134},{7,135},{8... | collective-permute-start | bytes 737288 | tf_op jit(solution)/shard_map/ppermute | solution.py:34
  45.8 5.5 %collective-permute-done.16 = bf16[2,2,48,640]{3,2,1,0:T(8,128)(2,1)S(1)} collective-permute-done((bf16[2,2,48,640]{3,2,1,0:T(8,128)(2,1)S(1)}, bf16[2,2,48,640]{3,2,1,0:T(8,128)(2,1)S(1)}, u32[]{:S(2)}, u32[]{:S(2)}) %collective-permute-start.16) | collective-permute-done | bytes 245792 | tf_op jit(solution)/shard_map/ppermute | solution.py:34
  51.3 0.1 pad_maximum_fusion.3
  51.4 8.5 %collective-permute-start.17 = (bf16[4,2,48,640]{3,2,1,0:T(8,128)(2,1)S(1)}, bf16[4,2,48,640]{3,2,1,0:T(8,128)(2,1)S(1)}, u32[]{:S(2)}, u32[]{:S(2)}) collective-permute-start(bf16[4,2,48,640]{3,2,1,0:T(8,128)(2,1)S(1)} %pad_maximum_fusion.3), channel_id=1, source_target_pairs={{0,64},{1,65},{2,66},{3,67},{4,68},{5,69},{6,70},{7,71},{8,72},{9,... | collective-permute-start | bytes 1474568 | tf_op jit(solution)/shard_map/ppermute | solution.py:34
  59.9 1.9 %collective-permute-start.2 = (bf16[2,48,640]{2,1,0:T(8,128)(2,1)S(1)}, bf16[2,48,640]{2,1,0:T(8,128)(2,1)S(1)}, u32[]{:S(2)}, u32[]{:S(2)}) collective-permute-start(bf16[2,48,640]{2,1,0:T(8,128)(2,1)S(1)} %bitcast.28), channel_id=1, source_target_pairs={{0,2},{1,3},{2,4},{3,5},{4,6},{5,7},{6,0},{7,1},{8,10},{9,11},{10,... | collective-permute-start | bytes 368648 | tf_op jit(solution)/shard_map/ppermute | solution.py:34
  61.8 10.0 %collective-permute-start.1 = (bf16[2,48,640]{2,1,0:T(8,128)(2,1)S(1)}, bf16[2,48,640]{2,1,0:T(8,128)(2,1)S(1)}, u32[]{:S(2)}, u32[]{:S(2)}) collective-permute-start(bf16[2,48,640]{2,1,0:T(8,128)(2,1)S(1)} %bitcast.29), channel_id=1, source_target_pairs={{0,4},{1,5},{2,6},{3,7},{4,0},{5,1},{6,2},{7,3},{8,12},{9,13},{10,... | collective-permute-start | bytes 368648 | tf_op jit(solution)/shard_map/ppermute | solution.py:34
  71.8 1.9 %collective-permute-start = (bf16[2,48,640]{2,1,0:T(8,128)(2,1)S(1)}, bf16[2,48,640]{2,1,0:T(8,128)(2,1)S(1)}, u32[]{:S(2)}, u32[]{:S(2)}) collective-permute-start(bf16[2,48,640]{2,1,0:T(8,128)(2,1)S(1)} %bitcast.30), channel_id=1, source_target_pairs={{0,6},{1,7},{2,0},{3,1},{4,2},{5,3},{6,4},{7,5},{8,14},{9,15},{10,... | collective-permute-start | bytes 368648 | tf_op jit(solution)/shard_map/ppermute | solution.py:34
  73.7 11.4 %collective-permute-start.6 = (bf16[2,48,640]{2,1,0:T(8,128)(2,1)S(1)}, bf16[2,48,640]{2,1,0:T(8,128)(2,1)S(1)}, u32[]{:S(2)}, u32[]{:S(2)}) collective-permute-start(bf16[2,48,640]{2,1,0:T(8,128)(2,1)S(1)} %bitcast.31), channel_id=1, source_target_pairs={{0,1},{1,0},{2,3},{3,2},{4,5},{5,4},{6,7},{7,6},{8,9},{9,8},{10,11... | collective-permute-start | bytes 368648 | tf_op jit(solution)/shard_map/ppermute | solution.py:34
  85.1 0.0 collective-permute-done.2
  85.1 0.0 collective-permute-done.1
  85.1 0.0 collective-permute-done
  85.1 0.1 pad_maximum_fusion.1.refs_0_
  85.2 1.9 %collective-permute-start.5 = (bf16[4,2,48,640]{3,2,1,0:T(8,128)(2,1)S(1)}, bf16[4,2,48,640]{3,2,1,0:T(8,128)(2,1)S(1)}, u32[]{:S(2)}, u32[]{:S(2)}) collective-permute-start(bf16[4,2,48,640]{3,2,1,0:T(8,128)(2,1)S(1)} %pad_maximum_fusion.1.refs_0_), channel_id=1, source_target_pairs={{0,8},{1,9},{2,10},{3,11},{4,12},{5,13},{6,14},{7,15},{8,16},{9,17... | collective-permute-start | bytes 1474568 | tf_op jit(solution)/shard_map/ppermute | solution.py:34
  87.2 2.6 %collective-permute-start.4 = (bf16[4,2,48,640]{3,2,1,0:T(8,128)(2,1)S(1)}, bf16[4,2,48,640]{3,2,1,0:T(8,128)(2,1)S(1)}, u32[]{:S(2)}, u32[]{:S(2)}) collective-permute-start(bf16[4,2,48,640]{3,2,1,0:T(8,128)(2,1)S(1)} %pad_maximum_fusion.1.refs_0_), channel_id=1, source_target_pairs={{0,16},{1,17},{2,18},{3,19},{4,20},{5,21},{6,22},{7,23},{8,24},{9,... | collective-permute-start | bytes 1474568 | tf_op jit(solution)/shard_map/ppermute | solution.py:34
  89.7 0.0 collective-permute-done.17
  89.8 0.1 pad_maximum_fusion.refs_8_
  89.9 6.1 %collective-permute-start.18 = (bf16[8,2,48,640]{3,2,1,0:T(8,128)(2,1)S(1)}, bf16[8,2,48,640]{3,2,1,0:T(8,128)(2,1)S(1)}, u32[]{:S(2)}, u32[]{:S(2)}) collective-permute-start(bf16[8,2,48,640]{3,2,1,0:T(8,128)(2,1)S(1)} %pad_maximum_fusion.refs_8_), channel_id=1, source_target_pairs={{0,32},{1,33},{2,34},{3,35},{4,36},{5,37},{6,38},{7,39},{8,40},{9,... | collective-permute-start | bytes 2949128 | tf_op jit(solution)/shard_map/ppermute | solution.py:34
  96.0 0.0 collective-permute-done.6
  96.0 1.9 %collective-permute-start.9 = (bf16[2,48,640]{2,1,0:T(8,128)(2,1)S(1)}, bf16[2,48,640]{2,1,0:T(8,128)(2,1)S(1)}, u32[]{:S(2)}, u32[]{:S(2)}) collective-permute-start(bf16[2,48,640]{2,1,0:T(8,128)(2,1)S(1)} %collective-permute-done.6), channel_id=1, source_target_pairs={{0,2},{1,3},{2,4},{3,5},{4,6},{5,7},{6,0},{7,1},{8,10},{9,11},{10,... | collective-permute-start | bytes 368648 | tf_op jit(solution)/shard_map/ppermute | solution.py:34
  98.0 1.9 %collective-permute-start.8 = (bf16[2,48,640]{2,1,0:T(8,128)(2,1)S(1)}, bf16[2,48,640]{2,1,0:T(8,128)(2,1)S(1)}, u32[]{:S(2)}, u32[]{:S(2)}) collective-permute-start(bf16[2,48,640]{2,1,0:T(8,128)(2,1)S(1)} %collective-permute-done.6), channel_id=1, source_target_pairs={{0,4},{1,5},{2,6},{3,7},{4,0},{5,1},{6,2},{7,3},{8,12},{9,13},{10,... | collective-permute-start | bytes 368648 | tf_op jit(solution)/shard_map/ppermute | solution.py:34
  99.9 7.4 %collective-permute-done.9 = bf16[2,48,640]{2,1,0:T(8,128)(2,1)S(1)} collective-permute-done((bf16[2,48,640]{2,1,0:T(8,128)(2,1)S(1)}, bf16[2,48,640]{2,1,0:T(8,128)(2,1)S(1)}, u32[]{:S(2)}, u32[]{:S(2)}) %collective-permute-start.9) | collective-permute-done | bytes 122912 | tf_op jit(solution)/shard_map/ppermute | solution.py:34
  107.3 1.9 %collective-permute-start.7 = (bf16[2,48,640]{2,1,0:T(8,128)(2,1)S(1)}, bf16[2,48,640]{2,1,0:T(8,128)(2,1)S(1)}, u32[]{:S(2)}, u32[]{:S(2)}) collective-permute-start(bf16[2,48,640]{2,1,0:T(8,128)(2,1)S(1)} %collective-permute-done.6), channel_id=1, source_target_pairs={{0,6},{1,7},{2,0},{3,1},{4,2},{5,3},{6,4},{7,5},{8,14},{9,15},{10,... | collective-permute-start | bytes 368648 | tf_op jit(solution)/shard_map/ppermute | solution.py:34
  109.2 0.0 collective-permute-done.8
  109.3 2.3 %collective-permute-start.3 = (bf16[4,2,48,640]{3,2,1,0:T(8,128)(2,1)S(1)}, bf16[4,2,48,640]{3,2,1,0:T(8,128)(2,1)}, u32[]{:S(2)}, u32[]{:S(2)}) collective-permute-start(bf16[4,2,48,640]{3,2,1,0:T(8,128)(2,1)S(1)} %pad_maximum_fusion.1.refs_0_), channel_id=1, source_target_pairs={{0,24},{1,25},{2,26},{3,27},{4,28},{5,29},{6,30},{7,31},{8,0},{9,1... | collective-permute-start | bytes 1474568 | tf_op jit(solution)/shard_map/ppermute | solution.py:34
  111.5 3.0 %collective-permute-done.7 = bf16[2,48,640]{2,1,0:T(8,128)(2,1)S(1)} collective-permute-done((bf16[2,48,640]{2,1,0:T(8,128)(2,1)S(1)}, bf16[2,48,640]{2,1,0:T(8,128)(2,1)S(1)}, u32[]{:S(2)}, u32[]{:S(2)}) %collective-permute-start.7) | collective-permute-done | bytes 122912 | tf_op jit(solution)/shard_map/ppermute | solution.py:34
  114.5 0.1 pad_maximum_fusion.2.refs_4_
  114.6 1.9 %collective-permute-start.12 = (bf16[4,2,48,640]{3,2,1,0:T(8,128)(2,1)S(1)}, bf16[4,2,48,640]{3,2,1,0:T(8,128)(2,1)}, u32[]{:S(2)}, u32[]{:S(2)}) collective-permute-start(bf16[4,2,48,640]{3,2,1,0:T(8,128)(2,1)S(1)} %pad_maximum_fusion.2.refs_4_), channel_id=1, source_target_pairs={{0,8},{1,9},{2,10},{3,11},{4,12},{5,13},{6,14},{7,15},{8,16},{9,17... | collective-permute-start | bytes 1474568 | tf_op jit(solution)/shard_map/ppermute | solution.py:34
  116.5 0.0 collective-permute-done.5.refs_3_
  116.5 4.1 %collective-permute-start.11 = (bf16[4,2,48,640]{3,2,1,0:T(8,128)(2,1)S(1)}, bf16[4,2,48,640]{3,2,1,0:T(8,128)(2,1)}, u32[]{:S(2)}, u32[]{:S(2)}) collective-permute-start(bf16[4,2,48,640]{3,2,1,0:T(8,128)(2,1)S(1)} %pad_maximum_fusion.2.refs_4_), channel_id=1, source_target_pairs={{0,16},{1,17},{2,18},{3,19},{4,20},{5,21},{6,22},{7,23},{8,24},{9,... | collective-permute-start | bytes 1474568 | tf_op jit(solution)/shard_map/ppermute | solution.py:34
  120.6 0.0 collective-permute-done.4.refs_2_
  120.6 0.0 copy-start
  120.7 0.8 copy-done
  121.4 4.0 %collective-permute-start.10 = (bf16[4,2,48,640]{3,2,1,0:T(8,128)(2,1)S(1)}, bf16[4,2,48,640]{3,2,1,0:T(8,128)(2,1)}, u32[]{:S(2)}, u32[]{:S(2)}) collective-permute-start(bf16[4,2,48,640]{3,2,1,0:T(8,128)(2,1)S(1)} %pad_maximum_fusion.2.refs_4_), channel_id=1, source_target_pairs={{0,24},{1,25},{2,26},{3,27},{4,28},{5,29},{6,30},{7,31},{8,0},{9,1... | collective-permute-start | bytes 1474568 | tf_op jit(solution)/shard_map/ppermute | solution.py:34
  125.4 0.1 pad_add_fusion.place
  125.5 0.0 collective-permute-done.3.refs_1_
  125.5 5.2 %collective-permute-done.12.refs_7_ = bf16[4,2,48,640]{3,2,1,0:T(8,128)(2,1)} collective-permute-done((bf16[4,2,48,640]{3,2,1,0:T(8,128)(2,1)S(1)}, bf16[4,2,48,640]{3,2,1,0:T(8,128)(2,1)}, u32[]{:S(2)}, u32[]{:S(2)}) %collective-permute-start.12) | collective-permute-done | bytes 491552 | tf_op jit(solution)/shard_map/ppermute | solution.py:34
  130.7 0.0 collective-permute-done.11.refs_6_
  130.7 2.5 %collective-permute-done.10.refs_5_ = bf16[4,2,48,640]{3,2,1,0:T(8,128)(2,1)} collective-permute-done((bf16[4,2,48,640]{3,2,1,0:T(8,128)(2,1)S(1)}, bf16[4,2,48,640]{3,2,1,0:T(8,128)(2,1)}, u32[]{:S(2)}, u32[]{:S(2)}) %collective-permute-start.10) | collective-permute-done | bytes 491552 | tf_op jit(solution)/shard_map/ppermute | solution.py:34
  133.2 0.0 collective-permute-done.18.refs_9_
  133.2 0.0 copy-start.1
  133.2 1.0 copy-done.1
  134.3 12.0 %shard_map.17 = f32[2,2,320,640]{3,2,1,0:T(8,128)} custom-call(s32[4]{0:T(128)S(1)} %pad_add_fusion.place, bf16[4,2,48,640]{3,2,1,0:T(8,128)(2,1)S(1)} %pad_maximum_fusion.1.refs_0_, bf16[4,2,48,640]{3,2,1,0:T(8,128)(2,1)} %collective-permute-done.3.refs_1_, bf16[4,2,48,640]{3,2,1,0:T(8,128)(2,1)S(1)} %copy-done.1, ...), custom_call_target="tpu_custom_call" | custom-call | tf_op jit(solution)/shard_map/pallas_call | solution.py:147
  (2 shorter events, 0.0 us)
Async XLA Ops:
  1.1 19.7 %collective-permute-start.13 = (bf16[48,640]{1,0:T(8,128)(2,1)S(1)}, bf16[48,640]{1,0:T(8,128)(2,1)S(1)}, u32[]{:S(2)}, u32[]{:S(2)}) collective-permute-start(bf16[48,640]{1,0:T(8,128)(2,1)S(1)} %get-tuple-element.5), channel_id=1, source_target_pairs={{0,0},{1,1},{2,32},{3,33},{4,64},{5,65},{6,96},{7,97},{8,128},{9,1... | collective-permute-start | bytes 184328 | tf_op jit(solution)/shard_map/ppermute | solution.py:34
  5.6 17.1 %collective-permute-start.14 = (bf16[48,640]{1,0:T(8,128)(2,1)S(1)}, bf16[48,640]{1,0:T(8,128)(2,1)S(1)}, u32[]{:S(2)}, u32[]{:S(2)}) collective-permute-start(bf16[48,640]{1,0:T(8,128)(2,1)S(1)} %get-tuple-element.6), channel_id=1, source_target_pairs={{0,1},{1,0},{2,33},{3,32},{4,65},{5,64},{6,97},{7,96},{8,129},{9,1... | collective-permute-start | bytes 184328 | tf_op jit(solution)/shard_map/ppermute | solution.py:34
  22.8 14.2 %collective-permute-start.15 = (bf16[1,2,48,640]{3,2,1,0:T(8,128)(2,1)S(1)}, bf16[1,2,48,640]{3,2,1,0:T(8,128)(2,1)S(1)}, u32[]{:S(2)}, u32[]{:S(2)}) collective-permute-start(bf16[1,2,48,640]{3,2,1,0:T(8,128)(2,1)S(1)} %maximum_bitcast_fusion), channel_id=1, source_target_pairs={{0,256},{1,257},{2,258},{3,259},{4,260},{5,261},{6,262},{7,263},{8... | collective-permute-start | bytes 368648 | tf_op jit(solution)/shard_map/ppermute | solution.py:34
  37.0 14.3 %collective-permute-start.16 = (bf16[2,2,48,640]{3,2,1,0:T(8,128)(2,1)S(1)}, bf16[2,2,48,640]{3,2,1,0:T(8,128)(2,1)S(1)}, u32[]{:S(2)}, u32[]{:S(2)}) collective-permute-start(bf16[2,2,48,640]{3,2,1,0:T(8,128)(2,1)S(1)} %pad_maximum_fusion.4), channel_id=1, source_target_pairs={{0,128},{1,129},{2,130},{3,131},{4,132},{5,133},{6,134},{7,135},{8... | collective-permute-start | bytes 737288 | tf_op jit(solution)/shard_map/ppermute | solution.py:34
  51.4 38.4 %collective-permute-start.17 = (bf16[4,2,48,640]{3,2,1,0:T(8,128)(2,1)S(1)}, bf16[4,2,48,640]{3,2,1,0:T(8,128)(2,1)S(1)}, u32[]{:S(2)}, u32[]{:S(2)}) collective-permute-start(bf16[4,2,48,640]{3,2,1,0:T(8,128)(2,1)S(1)} %pad_maximum_fusion.3), channel_id=1, source_target_pairs={{0,64},{1,65},{2,66},{3,67},{4,68},{5,69},{6,70},{7,71},{8,72},{9,... | collective-permute-start | bytes 1474568 | tf_op jit(solution)/shard_map/ppermute | solution.py:34
  59.9 25.2 %collective-permute-start.2 = (bf16[2,48,640]{2,1,0:T(8,128)(2,1)S(1)}, bf16[2,48,640]{2,1,0:T(8,128)(2,1)S(1)}, u32[]{:S(2)}, u32[]{:S(2)}) collective-permute-start(bf16[2,48,640]{2,1,0:T(8,128)(2,1)S(1)} %bitcast.28), channel_id=1, source_target_pairs={{0,2},{1,3},{2,4},{3,5},{4,6},{5,7},{6,0},{7,1},{8,10},{9,11},{10,... | collective-permute-start | bytes 368648 | tf_op jit(solution)/shard_map/ppermute | solution.py:34
  61.8 23.3 %collective-permute-start.1 = (bf16[2,48,640]{2,1,0:T(8,128)(2,1)S(1)}, bf16[2,48,640]{2,1,0:T(8,128)(2,1)S(1)}, u32[]{:S(2)}, u32[]{:S(2)}) collective-permute-start(bf16[2,48,640]{2,1,0:T(8,128)(2,1)S(1)} %bitcast.29), channel_id=1, source_target_pairs={{0,4},{1,5},{2,6},{3,7},{4,0},{5,1},{6,2},{7,3},{8,12},{9,13},{10,... | collective-permute-start | bytes 368648 | tf_op jit(solution)/shard_map/ppermute | solution.py:34
  71.8 13.3 %collective-permute-start = (bf16[2,48,640]{2,1,0:T(8,128)(2,1)S(1)}, bf16[2,48,640]{2,1,0:T(8,128)(2,1)S(1)}, u32[]{:S(2)}, u32[]{:S(2)}) collective-permute-start(bf16[2,48,640]{2,1,0:T(8,128)(2,1)S(1)} %bitcast.30), channel_id=1, source_target_pairs={{0,6},{1,7},{2,0},{3,1},{4,2},{5,3},{6,4},{7,5},{8,14},{9,15},{10,... | collective-permute-start | bytes 368648 | tf_op jit(solution)/shard_map/ppermute | solution.py:34
  73.7 22.3 %collective-permute-start.6 = (bf16[2,48,640]{2,1,0:T(8,128)(2,1)S(1)}, bf16[2,48,640]{2,1,0:T(8,128)(2,1)S(1)}, u32[]{:S(2)}, u32[]{:S(2)}) collective-permute-start(bf16[2,48,640]{2,1,0:T(8,128)(2,1)S(1)} %bitcast.31), channel_id=1, source_target_pairs={{0,1},{1,0},{2,3},{3,2},{4,5},{5,4},{6,7},{7,6},{8,9},{9,8},{10,11... | collective-permute-start | bytes 368648 | tf_op jit(solution)/shard_map/ppermute | solution.py:34
  85.2 31.3 %collective-permute-start.5 = (bf16[4,2,48,640]{3,2,1,0:T(8,128)(2,1)S(1)}, bf16[4,2,48,640]{3,2,1,0:T(8,128)(2,1)S(1)}, u32[]{:S(2)}, u32[]{:S(2)}) collective-permute-start(bf16[4,2,48,640]{3,2,1,0:T(8,128)(2,1)S(1)} %pad_maximum_fusion.1.refs_0_), channel_id=1, source_target_pairs={{0,8},{1,9},{2,10},{3,11},{4,12},{5,13},{6,14},{7,15},{8,16},{9,17... | collective-permute-start | bytes 1474568 | tf_op jit(solution)/shard_map/ppermute | solution.py:34
  87.2 33.5 %collective-permute-start.4 = (bf16[4,2,48,640]{3,2,1,0:T(8,128)(2,1)S(1)}, bf16[4,2,48,640]{3,2,1,0:T(8,128)(2,1)S(1)}, u32[]{:S(2)}, u32[]{:S(2)}) collective-permute-start(bf16[4,2,48,640]{3,2,1,0:T(8,128)(2,1)S(1)} %pad_maximum_fusion.1.refs_0_), channel_id=1, source_target_pairs={{0,16},{1,17},{2,18},{3,19},{4,20},{5,21},{6,22},{7,23},{8,24},{9,... | collective-permute-start | bytes 1474568 | tf_op jit(solution)/shard_map/ppermute | solution.py:34
  89.9 43.3 %collective-permute-start.18 = (bf16[8,2,48,640]{3,2,1,0:T(8,128)(2,1)S(1)}, bf16[8,2,48,640]{3,2,1,0:T(8,128)(2,1)S(1)}, u32[]{:S(2)}, u32[]{:S(2)}) collective-permute-start(bf16[8,2,48,640]{3,2,1,0:T(8,128)(2,1)S(1)} %pad_maximum_fusion.refs_8_), channel_id=1, source_target_pairs={{0,32},{1,33},{2,34},{3,35},{4,36},{5,37},{6,38},{7,39},{8,40},{9,... | collective-permute-start | bytes 2949128 | tf_op jit(solution)/shard_map/ppermute | solution.py:34
  96.0 11.3 %collective-permute-start.9 = (bf16[2,48,640]{2,1,0:T(8,128)(2,1)S(1)}, bf16[2,48,640]{2,1,0:T(8,128)(2,1)S(1)}, u32[]{:S(2)}, u32[]{:S(2)}) collective-permute-start(bf16[2,48,640]{2,1,0:T(8,128)(2,1)S(1)} %collective-permute-done.6), channel_id=1, source_target_pairs={{0,2},{1,3},{2,4},{3,5},{4,6},{5,7},{6,0},{7,1},{8,10},{9,11},{10,... | collective-permute-start | bytes 368648 | tf_op jit(solution)/shard_map/ppermute | solution.py:34
  98.0 11.3 %collective-permute-start.8 = (bf16[2,48,640]{2,1,0:T(8,128)(2,1)S(1)}, bf16[2,48,640]{2,1,0:T(8,128)(2,1)S(1)}, u32[]{:S(2)}, u32[]{:S(2)}) collective-permute-start(bf16[2,48,640]{2,1,0:T(8,128)(2,1)S(1)} %collective-permute-done.6), channel_id=1, source_target_pairs={{0,4},{1,5},{2,6},{3,7},{4,0},{5,1},{6,2},{7,3},{8,12},{9,13},{10,... | collective-permute-start | bytes 368648 | tf_op jit(solution)/shard_map/ppermute | solution.py:34
  107.3 7.2 %collective-permute-start.7 = (bf16[2,48,640]{2,1,0:T(8,128)(2,1)S(1)}, bf16[2,48,640]{2,1,0:T(8,128)(2,1)S(1)}, u32[]{:S(2)}, u32[]{:S(2)}) collective-permute-start(bf16[2,48,640]{2,1,0:T(8,128)(2,1)S(1)} %collective-permute-done.6), channel_id=1, source_target_pairs={{0,6},{1,7},{2,0},{3,1},{4,2},{5,3},{6,4},{7,5},{8,14},{9,15},{10,... | collective-permute-start | bytes 368648 | tf_op jit(solution)/shard_map/ppermute | solution.py:34
  109.3 16.2 %collective-permute-start.3 = (bf16[4,2,48,640]{3,2,1,0:T(8,128)(2,1)S(1)}, bf16[4,2,48,640]{3,2,1,0:T(8,128)(2,1)}, u32[]{:S(2)}, u32[]{:S(2)}) collective-permute-start(bf16[4,2,48,640]{3,2,1,0:T(8,128)(2,1)S(1)} %pad_maximum_fusion.1.refs_0_), channel_id=1, source_target_pairs={{0,24},{1,25},{2,26},{3,27},{4,28},{5,29},{6,30},{7,31},{8,0},{9,1... | collective-permute-start | bytes 1474568 | tf_op jit(solution)/shard_map/ppermute | solution.py:34
  114.6 16.2 %collective-permute-start.12 = (bf16[4,2,48,640]{3,2,1,0:T(8,128)(2,1)S(1)}, bf16[4,2,48,640]{3,2,1,0:T(8,128)(2,1)}, u32[]{:S(2)}, u32[]{:S(2)}) collective-permute-start(bf16[4,2,48,640]{3,2,1,0:T(8,128)(2,1)S(1)} %pad_maximum_fusion.2.refs_4_), channel_id=1, source_target_pairs={{0,8},{1,9},{2,10},{3,11},{4,12},{5,13},{6,14},{7,15},{8,16},{9,17... | collective-permute-start | bytes 1474568 | tf_op jit(solution)/shard_map/ppermute | solution.py:34
  116.5 14.2 %collective-permute-start.11 = (bf16[4,2,48,640]{3,2,1,0:T(8,128)(2,1)S(1)}, bf16[4,2,48,640]{3,2,1,0:T(8,128)(2,1)}, u32[]{:S(2)}, u32[]{:S(2)}) collective-permute-start(bf16[4,2,48,640]{3,2,1,0:T(8,128)(2,1)S(1)} %pad_maximum_fusion.2.refs_4_), channel_id=1, source_target_pairs={{0,16},{1,17},{2,18},{3,19},{4,20},{5,21},{6,22},{7,23},{8,24},{9,... | collective-permute-start | bytes 1474568 | tf_op jit(solution)/shard_map/ppermute | solution.py:34
  120.6 0.8 copy-start
  121.4 11.8 %collective-permute-start.10 = (bf16[4,2,48,640]{3,2,1,0:T(8,128)(2,1)S(1)}, bf16[4,2,48,640]{3,2,1,0:T(8,128)(2,1)}, u32[]{:S(2)}, u32[]{:S(2)}) collective-permute-start(bf16[4,2,48,640]{3,2,1,0:T(8,128)(2,1)S(1)} %pad_maximum_fusion.2.refs_4_), channel_id=1, source_target_pairs={{0,24},{1,25},{2,26},{3,27},{4,28},{5,29},{6,30},{7,31},{8,0},{9,1... | collective-permute-start | bytes 1474568 | tf_op jit(solution)/shard_map/ppermute | solution.py:34
  133.2 1.0 copy-start.1

commit v2 on v1

v2 whole, which is shorter than its diff:
```python
import functools
import math

import jax
import jax.numpy as jnp
from jax import lax
from jax.experimental import pallas as pl
from jax.experimental.pallas import tpu as pltpu
from jax.sharding import Mesh, PartitionSpec as P

water_factor = 0.5
tiny_eps = 1e-06

SIZES = dict(zl=8, core=2, y=4, x=4, zh=2)
AXES = tuple(SIZES)


def coordinates():
    out = [()]
    for size in SIZES.values():
        out = [c + (i,) for c in out for i in range(size)]
    return out


def number(c):
    n = 0
    for i, size in zip(c, SIZES.values()):
        n = n * size + i % size
    return n


def permute(value, target):
    pairs = [(number(c), number(target(*c))) for c in coordinates()]
    return lax.ppermute(value, AXES, pairs)


def fetch_first(value, offset):
    def target(zl, core, y, x, zh):
        return (zl, core, y, x - offset, zh) if core == 0 else (zl, core, y - offset, x, zh)

    return permute(value, target)


def fetch_second(value, offset):
    def target(zl, core, y, x, zh):
        return (zl, core, y - offset, x, zh) if core == 0 else (zl, core, y, x - offset, zh)

    return permute(value, target)


def gather_first(blocks):
    return jnp.stack([blocks] + [fetch_first(blocks, o) for o in (1, 2, 3)])


def gather_second(first):
    return [first] + [fetch_second(first, o) for o in (1, 2, 3)]


def to_column(value, cross):
    def target(zl, core, y, x, zh):
        s, g = zl * 2 + core, y * 4 + x
        return (g // 2, g % 2, s // 4, s % 4, 1 - zh if cross else zh)

    return permute(value, target)


def along_column(value, distance):
    return permute(value, lambda zl, core, y, x, zh: (zl ^ distance, core, y, x, zh))


def energy_of(block):
    values = block.astype(jnp.float32)
    half = values.shape[0] // 2
    real, imag = values[:half], values[half:]
    return real, imag, real * real + imag * imag


def fold(energy):
    return energy.reshape(energy.shape[0] // 8, 8, energy.shape[1]).sum(axis=0)


def floor_of(total, windows):
    return (water_factor / windows) * jnp.sum(total, axis=0, keepdims=True) + tiny_eps


def stacked(upper, lower):
    return jnp.concatenate([upper, lower], axis=0).astype(jnp.bfloat16)


def whiten_kernel(place, *refs):
    sources, wide = refs[:4], refs[4]
    core, y, x = place[1], place[2], place[3]
    freqs, rows, channels = sources[0].shape[2:]
    windows = 16 * rows
    for f in range(freqs):

        def add(a, total):
            for ref in sources:
                for zr in range(2):
                    total = total + fold(energy_of(ref[a, zr, f])[2])
            return total

        floor = floor_of(lax.fori_loop(0, 4, add, jnp.zeros((8, channels), jnp.float32)), windows)

        def whiten(a, carry):
            for second, ref in enumerate(sources):
                gy = lax.rem(y + jnp.where(core == 0, second, a), 4)
                gx = lax.rem(x + jnp.where(core == 0, a, second), 4)
                for zr in range(2):
                    real, imag, energy = energy_of(ref[a, zr, f])
                    scale = lax.rsqrt(energy + floor)
                    real, imag = real * scale, imag * scale
                    row = pl.multiple_of((zr * 16 + gy * 4 + gx) * rows, rows)
                    wide[f, pl.ds(row, rows), :channels] = stacked(real, imag)
                    wide[f, pl.ds(row, rows), channels:] = stacked(imag, -real)
            return carry

        lax.fori_loop(0, 4, whiten, 0)


def multiply_kernel(place, held, other, wide, arrived, out, left):
    del arrived
    zl, core = place[0], place[1]
    rows, channels = held.shape[2:]
    width = channels // 2
    windows = 16 * rows

    def add(a, total):
        for ref in (held, other):
            for zr in range(2):
                total = total + fold(energy_of(ref[a, zr])[2])
        return total

    floor = floor_of(lax.fori_loop(0, 8, add, jnp.zeros((8, channels), jnp.float32)), windows)

    def whiten(a, carry):
        along = lax.bitwise_xor(zl, (a % 2) * 4 + (a // 2 % 2) * 2 + a // 4)
        for n, ref in enumerate((held, other)):
            g = along * 2 + lax.bitwise_xor(core, n)
            for zr in range(2):
                real, imag, energy = energy_of(ref[a, zr])
                scale = lax.rsqrt(energy + floor)
                row = pl.multiple_of((zr * 16 + g) * rows, rows)
                block = stacked(real * scale, imag * scale)
                for f in range(2):
                    left[f, pl.ds(row, rows), :] = block[:, f * width : (f + 1) * width]
        return carry

    lax.fori_loop(0, 8, whiten, 0)
    stack_scale = 1.0 / math.sqrt(windows)
    for f in range(2):
        product = lax.dot_general(left[f], wide[f], (((0,), (0,)), ((), ())), preferred_element_type=jnp.float32)
        product = product * stack_scale
        out[0, f] = product[:, :channels]
        out[1, f] = product[:, channels:]


VMEM = pl.BlockSpec(memory_space=pltpu.VMEM)
SMEM = pl.BlockSpec(memory_space=pltpu.SMEM)


def whiten_sources(place, sources):
    freqs, rows, channels = sources[0].shape[2:]
    depth = 32 * rows
    return pl.pallas_call(
        whiten_kernel,
        out_shape=jax.ShapeDtypeStruct((freqs, depth, 2 * channels), jnp.bfloat16),
        in_specs=[SMEM] + [VMEM] * 4,
        out_specs=VMEM,
        compiler_params=pltpu.CompilerParams(vmem_limit_bytes=20 * 1024 * 1024),
        cost_estimate=pl.CostEstimate(flops=20 * depth * channels, bytes_accessed=8 * depth * channels, transcendentals=depth * channels),
    )(place, *sources)


def multiply(place, held, other, wide, arrived):
    rows, channels = held.shape[2:]
    depth = 32 * rows
    return pl.pallas_call(
        multiply_kernel,
        out_shape=jax.ShapeDtypeStruct((2, 2, channels // 2, channels), jnp.float32),
        in_specs=[SMEM] + [VMEM] * 4,
        out_specs=VMEM,
        scratch_shapes=[pltpu.VMEM((2, depth, channels // 2), jnp.bfloat16)],
        compiler_params=pltpu.CompilerParams(vmem_limit_bytes=20 * 1024 * 1024),
    )(place, held, other, wide, arrived)


def on_device(spectra):
    windows, _, freqs, channels = spectra.shape
    width = channels // 2
    place = jnp.stack([lax.axis_index(a) for a in ("zl", "core", "y", "x")]).astype(jnp.int32)
    zh = lax.axis_index("zh")
    block = jnp.transpose(spectra, (2, 1, 0, 3)).reshape(freqs, 2 * windows, channels)

    low = jnp.concatenate([block[0, :, :width], block[1, :, :width]], axis=1)
    high = jnp.concatenate([block[0, :, width:], block[1, :, width:]], axis=1)
    mine = jnp.where(zh == 0, low, high)
    theirs = jnp.where(zh == 0, high, low)
    held = jnp.stack([to_column(mine, False), to_column(theirs, True)])[None]
    partner = permute(block, lambda zl, core, y, x, zh: (zl, core, y, x, 1 - zh))
    held, partner = lax.optimization_barrier((held, partner))
    first = gather_first(jnp.stack([block, partner]))
    held = jnp.concatenate([held, along_column(held, 4)])
    held, first = lax.optimization_barrier((held, first))
    sources = gather_second(first)
    for distance in (2, 1):
        held = jnp.concatenate([held, along_column(held, distance)])
    arrived = jnp.stack([r[0, 0, 0, :16, :128] for r in sources[1:]])
    held, arrived = lax.optimization_barrier((held, arrived))
    wide = whiten_sources(place, sources)
    other = permute(held, lambda zl, core, y, x, zh: (zl, 1 - core, y, x, zh))

    crossed = multiply(place, held, other, wide, arrived)
    return jnp.transpose(crossed, (3, 0, 1, 2))


def solution(mesh):
    fine = Mesh(mesh.devices.reshape(tuple(SIZES.values())), AXES)
    return jax.shard_map(
        on_device,
        mesh=fine,
        in_specs=(P(("y", "x", "zh"), None, None, ("zl", "core")),),
        out_specs=P(("zl", "core"), None, None, ("y", "x", "zh")),
        check_vma=False,
    )
```

time: 147 us -> 120 us (0.82)
  starting transfers between devices: 102 us -> 74.5 us
  local copies, waits for them, and re-layouts: 2.81 us -> 5.33 us
  Pallas kernels: 12 us -> 10.1 us
    ppermute x19 -> x13, starting transfers between devices: 102 us -> 74.5 us  [permute(): return lax.ppermute(value, AXES, pairs)]
    unnamed x4 -> x8, local copies, waits for them, and re-layouts: 1.8 us -> 4.32 us
    pallas_call x1 -> x2, Pallas kernels: 12 us -> 10.1 us  [the longest x1 7.21 us: multiply(): pl.pallas_call(multiply_kernel, out_shape=jax.ShapeDtypeStruct((2, 2, cha...]
    ppermute x19 -> x13, waiting for transfers between devices: 28.8 us -> 28.4 us  [permute(): return lax.ppermute(value, AXES, pairs)]
  transfers between devices with their start and end apart: 19 -> 13, of which waited for: 7 -> 5; matrix products, arithmetic and copies ran while one was open for 0% -> 0% of each run, Pallas kernels for 0% -> 2%
where the time goes in v2:
time: 120 us; the launch traced here: 119 us
  starting transfers between devices  74.5 us (62%)
  waiting for transfers between devices  28.4 us (24%)
  Pallas kernels  10.1 us (8%)
  local copies, waits for them, and re-layouts  5.33 us (4%)
    ppermute x13, starting transfers between devices, permute(): return lax.ppermute(value, AXES, pairs)  74.5 us
    ppermute x13, waiting for transfers between devices, permute(): return lax.ppermute(value, AXES, pairs)  28.4 us
    pallas_call x1, Pallas kernels, multiply(): pl.pallas_call(multiply_kernel, out_shape=jax.ShapeDtypeStruct((2, 2, cha...  7.21 us
    unnamed x8, local copies, waits for them, and re-layouts  4.32 us
    pallas_call x1, Pallas kernels, whiten_sources(): pl.pallas_call(whiten_kernel, out_shape=jax.ShapeDtypeStruct((freqs, dept...  2.9 us
  transfers between devices with their start and end apart: 13, of which 5 were waited for; matrix products, arithmetic and copies ran while one was open for 0% of the time, Pallas kernels for 2%

profile of v2, /device:TPU:1, one launch (start us, length us, event | category | flops | bytes accessed | tf_op | source)
XLA Modules:
  0.0 119.2 jit_solution(12665553097335112777)
XLA Ops:
  0.0 0.9 copy.2
  0.9 0.1 slice_bitcast_fusion.3
  1.0 0.1 broadcast_select_fusion.1
  1.1 4.5 %collective-permute-start = (bf16[48,640]{1,0:T(8,128)(2,1)S(1)}, bf16[48,640]{1,0:T(8,128)(2,1)S(1)}, u32[]{:S(2)}, u32[]{:S(2)}) collective-permute-start(bf16[48,640]{1,0:T(8,128)(2,1)S(1)} %get-tuple-element.19), channel_id=1, source_target_pairs={{0,0},{1,1},{2,32},{3,33},{4,64},{5,65},{6,96},{7,97},{8,128},{9,1... | collective-permute-start | bytes 184328 | tf_op jit(solution)/shard_map/ppermute | solution.py:34
  5.6 15.2 %collective-permute-start.1 = (bf16[48,640]{1,0:T(8,128)(2,1)S(1)}, bf16[48,640]{1,0:T(8,128)(2,1)S(1)}, u32[]{:S(2)}, u32[]{:S(2)}) collective-permute-start(bf16[48,640]{1,0:T(8,128)(2,1)S(1)} %get-tuple-element.20), channel_id=1, source_target_pairs={{0,1},{1,0},{2,33},{3,32},{4,65},{5,64},{6,97},{7,96},{8,129},{9,1... | collective-permute-start | bytes 184328 | tf_op jit(solution)/shard_map/ppermute | solution.py:34
  20.8 2.2 %collective-permute-start.2 = (bf16[2,48,640]{2,1,0:T(8,128)(2,1)S(1)}, bf16[2,48,640]{2,1,0:T(8,128)(2,1)S(1)}, u32[]{:S(2)}, u32[]{:S(2)}) collective-permute-start(bf16[2,48,640]{2,1,0:T(8,128)(2,1)S(1)} %bitcast.33), channel_id=1, source_target_pairs={{0,1},{1,0},{2,3},{3,2},{4,5},{5,4},{6,7},{7,6},{8,9},{9,8},{10,11... | collective-permute-start | bytes 368648 | tf_op jit(solution)/shard_map/ppermute | solution.py:34
  23.0 0.0 collective-permute-done
  23.0 0.0 collective-permute-done.1
  23.1 12.4 %collective-permute-done.2 = bf16[2,48,640]{2,1,0:T(8,128)(2,1)S(1)} collective-permute-done((bf16[2,48,640]{2,1,0:T(8,128)(2,1)S(1)}, bf16[2,48,640]{2,1,0:T(8,128)(2,1)S(1)}, u32[]{:S(2)}, u32[]{:S(2)}) %collective-permute-start.2) | collective-permute-done | bytes 122912 | tf_op jit(solution)/shard_map/ppermute | solution.py:34
  35.5 10.7 %collective-permute-start.4 = (bf16[2,2,48,640]{3,2,1,0:T(8,128)(2,1)S(1)}, bf16[2,2,48,640]{3,2,1,0:T(8,128)(2,1)S(1)}, u32[]{:S(2)}, u32[]{:S(2)}) collective-permute-start(bf16[2,2,48,640]{3,2,1,0:T(8,128)(2,1)S(1)} %get-tuple-element.18), channel_id=1, source_target_pairs={{0,6},{1,7},{2,0},{3,1},{4,2},{5,3},{6,4},{7,5},{8,14},{9,15},{10,... | collective-permute-start | bytes 737288 | tf_op jit(solution)/shard_map/ppermute | solution.py:34
  46.2 1.9 %collective-permute-start.5 = (bf16[2,2,48,640]{3,2,1,0:T(8,128)(2,1)S(1)}, bf16[2,2,48,640]{3,2,1,0:T(8,128)(2,1)S(1)}, u32[]{:S(2)}, u32[]{:S(2)}) collective-permute-start(bf16[2,2,48,640]{3,2,1,0:T(8,128)(2,1)S(1)} %get-tuple-element.18), channel_id=1, source_target_pairs={{0,4},{1,5},{2,6},{3,7},{4,0},{5,1},{6,2},{7,3},{8,12},{9,13},{10,... | collective-permute-start | bytes 737288 | tf_op jit(solution)/shard_map/ppermute | solution.py:34
  48.1 2.5 %collective-permute-start.6 = (bf16[2,2,48,640]{3,2,1,0:T(8,128)(2,1)S(1)}, bf16[2,2,48,640]{3,2,1,0:T(8,128)(2,1)S(1)}, u32[]{:S(2)}, u32[]{:S(2)}) collective-permute-start(bf16[2,2,48,640]{3,2,1,0:T(8,128)(2,1)S(1)} %get-tuple-element.18), channel_id=1, source_target_pairs={{0,2},{1,3},{2,4},{3,5},{4,6},{5,7},{6,0},{7,1},{8,10},{9,11},{10,... | collective-permute-start | bytes 737288 | tf_op jit(solution)/shard_map/ppermute | solution.py:34
  50.6 7.9 %collective-permute-start.3 = (bf16[1,2,48,640]{3,2,1,0:T(8,128)(2,1)S(1)}, bf16[1,2,48,640]{3,2,1,0:T(8,128)(2,1)S(1)}, u32[]{:S(2)}, u32[]{:S(2)}) collective-permute-start(bf16[1,2,48,640]{3,2,1,0:T(8,128)(2,1)S(1)} %maximum_bitcast_fusion), channel_id=1, source_target_pairs={{0,256},{1,257},{2,258},{3,259},{4,260},{5,261},{6,262},{7,263},{8... | collective-permute-start | bytes 368648 | tf_op jit(solution)/shard_map/ppermute | solution.py:34
  58.5 3.1 %collective-permute-done.3 = bf16[1,2,48,640]{3,2,1,0:T(8,128)(2,1)S(1)} collective-permute-done((bf16[1,2,48,640]{3,2,1,0:T(8,128)(2,1)S(1)}, bf16[1,2,48,640]{3,2,1,0:T(8,128)(2,1)S(1)}, u32[]{:S(2)}, u32[]{:S(2)}) %collective-permute-start.3) | collective-permute-done | bytes 122912 | tf_op jit(solution)/shard_map/ppermute | solution.py:34
  61.7 0.0 collective-permute-done.4
  61.7 0.0 collective-permute-done.5
  61.7 0.0 collective-permute-done.6
  61.7 0.1 pad_maximum_fusion.refs_0_
  61.9 8.3 %collective-permute-start.7 = (bf16[2,2,48,640]{3,2,1,0:T(8,128)(2,1)S(1)}, bf16[2,2,48,640]{3,2,1,0:T(8,128)(2,1)S(1)}, u32[]{:S(2)}, u32[]{:S(2)}) collective-permute-start(bf16[2,2,48,640]{3,2,1,0:T(8,128)(2,1)S(1)} %pad_maximum_fusion.3), channel_id=1, source_target_pairs={{0,128},{1,129},{2,130},{3,131},{4,132},{5,133},{6,134},{7,135},{8... | collective-permute-start | bytes 737288 | tf_op jit(solution)/shard_map/ppermute | solution.py:34
  70.2 3.5 %collective-permute-start.11 = (bf16[4,2,2,48,640]{4,3,2,1,0:T(8,128)(2,1)S(1)}, bf16[4,2,2,48,640]{4,3,2,1,0:T(8,128)(2,1)S(1)}, u32[]{:S(2)}, u32[]{:S(2)}) collective-permute-start(bf16[4,2,2,48,640]{4,3,2,1,0:T(8,128)(2,1)S(1)} %pad_maximum_fusion.refs_0_), channel_id=1, source_target_pairs={{0,8},{1,9},{2,10},{3,11},{4,12},{5,13},{6,14},{7,15},{8,16},{9,17... | collective-permute-start | bytes 2949128 | tf_op jit(solution)/shard_map/ppermute | solution.py:34
  73.7 6.0 %collective-permute-start.10 = (bf16[4,2,2,48,640]{4,3,2,1,0:T(8,128)(2,1)S(1)}, bf16[4,2,2,48,640]{4,3,2,1,0:T(8,128)(2,1)S(1)}, u32[]{:S(2)}, u32[]{:S(2)}) collective-permute-start(bf16[4,2,2,48,640]{4,3,2,1,0:T(8,128)(2,1)S(1)} %pad_maximum_fusion.refs_0_), channel_id=1, source_target_pairs={{0,16},{1,17},{2,18},{3,19},{4,20},{5,21},{6,22},{7,23},{8,24},{9,... | collective-permute-start | bytes 2949128 | tf_op jit(solution)/shard_map/ppermute | solution.py:34
  79.8 0.0 collective-permute-done.7
  79.8 0.1 pad_maximum_fusion.2
  79.8 4.5 %collective-permute-start.8 = (bf16[4,2,48,640]{3,2,1,0:T(8,128)(2,1)S(1)}, bf16[4,2,48,640]{3,2,1,0:T(8,128)(2,1)S(1)}, u32[]{:S(2)}, u32[]{:S(2)}) collective-permute-start(bf16[4,2,48,640]{3,2,1,0:T(8,128)(2,1)S(1)} %pad_maximum_fusion.2), channel_id=1, source_target_pairs={{0,64},{1,65},{2,66},{3,67},{4,68},{5,69},{6,70},{7,71},{8,72},{9,... | collective-permute-start | bytes 1474568 | tf_op jit(solution)/shard_map/ppermute | solution.py:34
  84.3 3.5 %collective-permute-start.9 = (bf16[4,2,2,48,640]{4,3,2,1,0:T(8,128)(2,1)S(1)}, bf16[4,2,2,48,640]{4,3,2,1,0:T(8,128)(2,1)S(1)}, u32[]{:S(2)}, u32[]{:S(2)}) collective-permute-start(bf16[4,2,2,48,640]{4,3,2,1,0:T(8,128)(2,1)S(1)} %pad_maximum_fusion.refs_0_), channel_id=1, source_target_pairs={{0,24},{1,25},{2,26},{3,27},{4,28},{5,29},{6,30},{7,31},{8,0},{9,1... | collective-permute-start | bytes 2949128 | tf_op jit(solution)/shard_map/ppermute | solution.py:34
  87.8 6.6 %collective-permute-done.8 = bf16[4,2,48,640]{3,2,1,0:T(8,128)(2,1)S(1)} collective-permute-done((bf16[4,2,48,640]{3,2,1,0:T(8,128)(2,1)S(1)}, bf16[4,2,48,640]{3,2,1,0:T(8,128)(2,1)S(1)}, u32[]{:S(2)}, u32[]{:S(2)}) %collective-permute-start.8) | collective-permute-done | bytes 491552 | tf_op jit(solution)/shard_map/ppermute | solution.py:34
  94.4 0.1 pad_maximum_fusion.1.held
  94.5 0.0 collective-permute-done.11.refs_3_
  94.5 5.6 %collective-permute-done.10.refs_2_ = bf16[4,2,2,48,640]{4,3,2,1,0:T(8,128)(2,1)S(1)} collective-permute-done((bf16[4,2,2,48,640]{4,3,2,1,0:T(8,128)(2,1)S(1)}, bf16[4,2,2,48,640]{4,3,2,1,0:T(8,128)(2,1)S(1)}, u32[]{:S(2)}, u32[]{:S(2)}) %collective-permute-start.10) | collective-permute-done | bytes 983072 | tf_op jit(solution)/shard_map/ppermute | solution.py:34
  100.1 0.0 copy-start
  100.1 1.0 copy-done
  101.1 0.7 collective-permute-done.9.refs_1_
  101.8 0.0 copy-start.2
  101.8 0.9 copy-done.2
  102.7 3.9 %collective-permute-start.12 = (bf16[8,2,48,640]{3,2,1,0:T(8,128)(2,1)S(1)}, bf16[8,2,48,640]{3,2,1,0:T(8,128)(2,1)}, u32[]{:S(2)}, u32[]{:S(2)}) collective-permute-start(bf16[8,2,48,640]{3,2,1,0:T(8,128)(2,1)S(1)} %pad_maximum_fusion.1.held), channel_id=1, source_target_pairs={{0,32},{1,33},{2,34},{3,35},{4,36},{5,37},{6,38},{7,39},{8,40},{9,... | collective-permute-start | bytes 2949128 | tf_op jit(solution)/shard_map/ppermute | solution.py:34
  106.6 0.1 pad_add_fusion.place
  106.7 0.0 copy-start.1
  106.7 1.2 %copy-done.1 = bf16[4,2,2,48,640]{4,3,2,1,0:T(8,128)(2,1)S(1)} copy-done((bf16[4,2,2,48,640]{4,3,2,1,0:T(8,128)(2,1)S(1)}, bf16[4,2,2,48,640]{4,3,2,1,0:T(8,128)(2,1)}, u32[]{:S(2)}) %copy-start.1) | copy-done | bytes 983064
  107.9 0.0 copy-start.3
  107.9 1.2 %copy-done.3 = bf16[4,2,2,48,640]{4,3,2,1,0:T(8,128)(2,1)S(1)} copy-done((bf16[4,2,2,48,640]{4,3,2,1,0:T(8,128)(2,1)S(1)}, bf16[4,2,2,48,640]{4,3,2,1,0:T(8,128)(2,1)}, u32[]{:S(2)}) %copy-start.3) | copy-done | bytes 983064
  109.1 2.9 %shard_map.17.wide = bf16[2,1536,1280]{2,1,0:T(8,128)(2,1)S(1)} custom-call(s32[4]{0:T(128)S(1)} %pad_add_fusion.place, bf16[4,2,2,48,640]{4,3,2,1,0:T(8,128)(2,1)S(1)} %pad_maximum_fusion.refs_0_, bf16[4,2,2,48,640]{4,3,2,1,0:T(8,128)(2,1)S(1)} %copy-done.3, bf16[4,2,2,48,640]{4,3,2,1,0:T(8,128)(2,1)S(1)} %copy-done.1, ...), custom_call_target="tpu_custom_call" | custom-call | flops 19660800 | bytes 7864320 | tf_op jit(solution)/shard_map/pallas_call | solution.py:165
  112.0 0.0 collective-permute-done.12.other
  112.0 7.2 %shard_map.18 = f32[2,2,320,640]{3,2,1,0:T(8,128)} custom-call(s32[4]{0:T(128)S(1)} %pad_add_fusion.place, bf16[8,2,48,640]{3,2,1,0:T(8,128)(2,1)S(1)} %pad_maximum_fusion.1.held, bf16[8,2,48,640]{3,2,1,0:T(8,128)(2,1)} %collective-permute-done.12.other, bf16[2,1536,1280]{2,1,0:T(8,128)(2,1)S(1)} %shard_map.17.wide, ...), custom_call_target="tpu_custom_call" | custom-call | tf_op jit(solution)/shard_map/pallas_call | solution.py:178
  (7 shorter events, 0.1 us)
Async XLA Ops:
  1.1 21.9 %collective-permute-start = (bf16[48,640]{1,0:T(8,128)(2,1)S(1)}, bf16[48,640]{1,0:T(8,128)(2,1)S(1)}, u32[]{:S(2)}, u32[]{:S(2)}) collective-permute-start(bf16[48,640]{1,0:T(8,128)(2,1)S(1)} %get-tuple-element.19), channel_id=1, source_target_pairs={{0,0},{1,1},{2,32},{3,33},{4,64},{5,65},{6,96},{7,97},{8,128},{9,1... | collective-permute-start | bytes 184328 | tf_op jit(solution)/shard_map/ppermute | solution.py:34
  5.6 17.4 %collective-permute-start.1 = (bf16[48,640]{1,0:T(8,128)(2,1)S(1)}, bf16[48,640]{1,0:T(8,128)(2,1)S(1)}, u32[]{:S(2)}, u32[]{:S(2)}) collective-permute-start(bf16[48,640]{1,0:T(8,128)(2,1)S(1)} %get-tuple-element.20), channel_id=1, source_target_pairs={{0,1},{1,0},{2,33},{3,32},{4,65},{5,64},{6,97},{7,96},{8,129},{9,1... | collective-permute-start | bytes 184328 | tf_op jit(solution)/shard_map/ppermute | solution.py:34
  20.8 14.6 %collective-permute-start.2 = (bf16[2,48,640]{2,1,0:T(8,128)(2,1)S(1)}, bf16[2,48,640]{2,1,0:T(8,128)(2,1)S(1)}, u32[]{:S(2)}, u32[]{:S(2)}) collective-permute-start(bf16[2,48,640]{2,1,0:T(8,128)(2,1)S(1)} %bitcast.33), channel_id=1, source_target_pairs={{0,1},{1,0},{2,3},{3,2},{4,5},{5,4},{6,7},{7,6},{8,9},{9,8},{10,11... | collective-permute-start | bytes 368648 | tf_op jit(solution)/shard_map/ppermute | solution.py:34
  35.5 26.2 %collective-permute-start.4 = (bf16[2,2,48,640]{3,2,1,0:T(8,128)(2,1)S(1)}, bf16[2,2,48,640]{3,2,1,0:T(8,128)(2,1)S(1)}, u32[]{:S(2)}, u32[]{:S(2)}) collective-permute-start(bf16[2,2,48,640]{3,2,1,0:T(8,128)(2,1)S(1)} %get-tuple-element.18), channel_id=1, source_target_pairs={{0,6},{1,7},{2,0},{3,1},{4,2},{5,3},{6,4},{7,5},{8,14},{9,15},{10,... | collective-permute-start | bytes 737288 | tf_op jit(solution)/shard_map/ppermute | solution.py:34
  46.2 15.5 %collective-permute-start.5 = (bf16[2,2,48,640]{3,2,1,0:T(8,128)(2,1)S(1)}, bf16[2,2,48,640]{3,2,1,0:T(8,128)(2,1)S(1)}, u32[]{:S(2)}, u32[]{:S(2)}) collective-permute-start(bf16[2,2,48,640]{3,2,1,0:T(8,128)(2,1)S(1)} %get-tuple-element.18), channel_id=1, source_target_pairs={{0,4},{1,5},{2,6},{3,7},{4,0},{5,1},{6,2},{7,3},{8,12},{9,13},{10,... | collective-permute-start | bytes 737288 | tf_op jit(solution)/shard_map/ppermute | solution.py:34
  48.1 13.6 %collective-permute-start.6 = (bf16[2,2,48,640]{3,2,1,0:T(8,128)(2,1)S(1)}, bf16[2,2,48,640]{3,2,1,0:T(8,128)(2,1)S(1)}, u32[]{:S(2)}, u32[]{:S(2)}) collective-permute-start(bf16[2,2,48,640]{3,2,1,0:T(8,128)(2,1)S(1)} %get-tuple-element.18), channel_id=1, source_target_pairs={{0,2},{1,3},{2,4},{3,5},{4,6},{5,7},{6,0},{7,1},{8,10},{9,11},{10,... | collective-permute-start | bytes 737288 | tf_op jit(solution)/shard_map/ppermute | solution.py:34
  50.6 11.0 %collective-permute-start.3 = (bf16[1,2,48,640]{3,2,1,0:T(8,128)(2,1)S(1)}, bf16[1,2,48,640]{3,2,1,0:T(8,128)(2,1)S(1)}, u32[]{:S(2)}, u32[]{:S(2)}) collective-permute-start(bf16[1,2,48,640]{3,2,1,0:T(8,128)(2,1)S(1)} %maximum_bitcast_fusion), channel_id=1, source_target_pairs={{0,256},{1,257},{2,258},{3,259},{4,260},{5,261},{6,262},{7,263},{8... | collective-permute-start | bytes 368648 | tf_op jit(solution)/shard_map/ppermute | solution.py:34
  61.9 17.9 %collective-permute-start.7 = (bf16[2,2,48,640]{3,2,1,0:T(8,128)(2,1)S(1)}, bf16[2,2,48,640]{3,2,1,0:T(8,128)(2,1)S(1)}, u32[]{:S(2)}, u32[]{:S(2)}) collective-permute-start(bf16[2,2,48,640]{3,2,1,0:T(8,128)(2,1)S(1)} %pad_maximum_fusion.3), channel_id=1, source_target_pairs={{0,128},{1,129},{2,130},{3,131},{4,132},{5,133},{6,134},{7,135},{8... | collective-permute-start | bytes 737288 | tf_op jit(solution)/shard_map/ppermute | solution.py:34
  70.2 24.3 %collective-permute-start.11 = (bf16[4,2,2,48,640]{4,3,2,1,0:T(8,128)(2,1)S(1)}, bf16[4,2,2,48,640]{4,3,2,1,0:T(8,128)(2,1)S(1)}, u32[]{:S(2)}, u32[]{:S(2)}) collective-permute-start(bf16[4,2,2,48,640]{4,3,2,1,0:T(8,128)(2,1)S(1)} %pad_maximum_fusion.refs_0_), channel_id=1, source_target_pairs={{0,8},{1,9},{2,10},{3,11},{4,12},{5,13},{6,14},{7,15},{8,16},{9,17... | collective-permute-start | bytes 2949128 | tf_op jit(solution)/shard_map/ppermute | solution.py:34
  73.7 26.4 %collective-permute-start.10 = (bf16[4,2,2,48,640]{4,3,2,1,0:T(8,128)(2,1)S(1)}, bf16[4,2,2,48,640]{4,3,2,1,0:T(8,128)(2,1)S(1)}, u32[]{:S(2)}, u32[]{:S(2)}) collective-permute-start(bf16[4,2,2,48,640]{4,3,2,1,0:T(8,128)(2,1)S(1)} %pad_maximum_fusion.refs_0_), channel_id=1, source_target_pairs={{0,16},{1,17},{2,18},{3,19},{4,20},{5,21},{6,22},{7,23},{8,24},{9,... | collective-permute-start | bytes 2949128 | tf_op jit(solution)/shard_map/ppermute | solution.py:34
  79.8 14.5 %collective-permute-start.8 = (bf16[4,2,48,640]{3,2,1,0:T(8,128)(2,1)S(1)}, bf16[4,2,48,640]{3,2,1,0:T(8,128)(2,1)S(1)}, u32[]{:S(2)}, u32[]{:S(2)}) collective-permute-start(bf16[4,2,48,640]{3,2,1,0:T(8,128)(2,1)S(1)} %pad_maximum_fusion.2), channel_id=1, source_target_pairs={{0,64},{1,65},{2,66},{3,67},{4,68},{5,69},{6,70},{7,71},{8,72},{9,... | collective-permute-start | bytes 1474568 | tf_op jit(solution)/shard_map/ppermute | solution.py:34
  84.3 17.5 %collective-permute-start.9 = (bf16[4,2,2,48,640]{4,3,2,1,0:T(8,128)(2,1)S(1)}, bf16[4,2,2,48,640]{4,3,2,1,0:T(8,128)(2,1)S(1)}, u32[]{:S(2)}, u32[]{:S(2)}) collective-permute-start(bf16[4,2,2,48,640]{4,3,2,1,0:T(8,128)(2,1)S(1)} %pad_maximum_fusion.refs_0_), channel_id=1, source_target_pairs={{0,24},{1,25},{2,26},{3,27},{4,28},{5,29},{6,30},{7,31},{8,0},{9,1... | collective-permute-start | bytes 2949128 | tf_op jit(solution)/shard_map/ppermute | solution.py:34
  100.1 1.0 copy-start
  101.8 0.9 copy-start.2
  102.7 9.3 %collective-permute-start.12 = (bf16[8,2,48,640]{3,2,1,0:T(8,128)(2,1)S(1)}, bf16[8,2,48,640]{3,2,1,0:T(8,128)(2,1)}, u32[]{:S(2)}, u32[]{:S(2)}) collective-permute-start(bf16[8,2,48,640]{3,2,1,0:T(8,128)(2,1)S(1)} %pad_maximum_fusion.1.held), channel_id=1, source_target_pairs={{0,32},{1,33},{2,34},{3,35},{4,36},{5,37},{6,38},{7,39},{8,40},{9,... | collective-permute-start | bytes 2949128 | tf_op jit(solution)/shard_map/ppermute | solution.py:34
  106.7 1.2 %copy-start.1 = (bf16[4,2,2,48,640]{4,3,2,1,0:T(8,128)(2,1)S(1)}, bf16[4,2,2,48,640]{4,3,2,1,0:T(8,128)(2,1)}, u32[]{:S(2)}) copy-start(bf16[4,2,2,48,640]{4,3,2,1,0:T(8,128)(2,1)} %copy-done) | copy-start | bytes 2949124
  107.9 1.2 %copy-start.3 = (bf16[4,2,2,48,640]{4,3,2,1,0:T(8,128)(2,1)S(1)}, bf16[4,2,2,48,640]{4,3,2,1,0:T(8,128)(2,1)}, u32[]{:S(2)}) copy-start(bf16[4,2,2,48,640]{4,3,2,1,0:T(8,128)(2,1)} %copy-done.2) | copy-start | bytes 2949124

commit v3 on v2

v3 whole, which is shorter than its diff:
```python
import functools
import math

import jax
import jax.numpy as jnp
from jax import lax
from jax.experimental import pallas as pl
from jax.experimental.pallas import tpu as pltpu
from jax.sharding import Mesh, PartitionSpec as P

water_factor = 0.5
tiny_eps = 1e-06

SIZES = dict(zl=8, core=2, y=4, x=4, zh=2)
AXES = tuple(SIZES)


def coordinates():
    out = [()]
    for size in SIZES.values():
        out = [c + (i,) for c in out for i in range(size)]
    return out


def number(c):
    n = 0
    for i, size in zip(c, SIZES.values()):
        n = n * size + i % size
    return n


def permute(value, target):
    pairs = [(number(c), number(target(*c))) for c in coordinates()]
    return lax.ppermute(value, AXES, pairs)


def groups_of(swapped):
    along_x = [[[c * 16 + y * 4 + x for x in range(4)] for y in range(4)] for c in range(2)]
    along_y = [[[c * 16 + y * 4 + x for y in range(4)] for x in range(4)] for c in range(2)]
    return along_y[0] + along_x[1] if swapped else along_x[0] + along_y[1]


def gather_four(value, swapped):
    copies = jnp.broadcast_to(value, (4,) + value.shape)
    return lax.all_to_all(copies, ("core", "y", "x"), 0, 0, axis_index_groups=groups_of(swapped))


def to_column(value, copy, cross):
    def target(zl, core, y, x, zh):
        s, g = zl * 2 + core, y * 4 + x
        group, slot = (g + copy) % 2, g // 2
        return (group * 4 + slot // 2, slot % 2, s // 4, s % 4, 1 - zh if cross else zh)

    return permute(value, target)


def along_column(value, distance):
    return permute(value, lambda zl, core, y, x, zh: (zl ^ distance, core, y, x, zh))


def energy_of(block):
    values = block.astype(jnp.float32)
    half = values.shape[0] // 2
    real, imag = values[:half], values[half:]
    return real, imag, real * real + imag * imag


def fold(energy):
    return energy.reshape(energy.shape[0] // 8, 8, energy.shape[1]).sum(axis=0)


def floor_of(total, windows):
    return (water_factor / windows) * jnp.sum(total, axis=0, keepdims=True) + tiny_eps


def stacked(upper, lower):
    return jnp.concatenate([upper, lower], axis=0).astype(jnp.bfloat16)


def whiten_kernel(place, *refs):
    sources, wide = refs
    core = place[1]
    freqs, rows, channels = sources.shape[3:]
    windows = 16 * rows
    for f in range(freqs):

        def add(second, total):
            for first in range(4):
                for zr in range(2):
                    total = total + fold(energy_of(sources[second, first, zr, f])[2])
            return total

        floor = floor_of(lax.fori_loop(0, 4, add, jnp.zeros((8, channels), jnp.float32)), windows)

        def whiten(second, carry):
            for first in range(4):
                g = jnp.where(core == 0, second * 4 + first, first * 4 + second)
                for zr in range(2):
                    real, imag, energy = energy_of(sources[second, first, zr, f])
                    scale = lax.rsqrt(energy + floor)
                    real, imag = real * scale, imag * scale
                    row = pl.multiple_of((zr * 16 + g) * rows, rows)
                    wide[f, pl.ds(row, rows), :channels] = stacked(real, imag)
                    wide[f, pl.ds(row, rows), channels:] = stacked(imag, -real)
            return carry

        lax.fori_loop(0, 4, whiten, 0)


def multiply_kernel(place, held, other, wide, out, left):
    zl, core = place[0], place[1]
    rows, channels = held.shape[2:]
    width = channels // 2
    windows = 16 * rows

    @pl.when(pl.program_id(0) == 0)
    def _():
        def add(a, total):
            for ref in (held, other):
                for zr in range(2):
                    total = total + fold(energy_of(ref[a, zr])[2])
            return total

        floor = floor_of(lax.fori_loop(0, 8, add, jnp.zeros((8, channels), jnp.float32)), windows)

        def whiten(a, carry):
            along = lax.rem(lax.bitwise_xor(zl, a // 2), 4)
            copy = lax.rem(zl // 4 + a, 2)
            for n, ref in enumerate((held, other)):
                g = along * 4 + lax.bitwise_xor(core, n) * 2 + copy
                for zr in range(2):
                    real, imag, energy = energy_of(ref[a, zr])
                    scale = lax.rsqrt(energy + floor)
                    row = pl.multiple_of((zr * 16 + g) * rows, rows)
                    block = stacked(real * scale, imag * scale)
                    for f in range(2):
                        left[f, pl.ds(row, rows), :] = block[:, f * width : (f + 1) * width]
            return carry

        lax.fori_loop(0, 8, whiten, 0)

    stack_scale = 1.0 / math.sqrt(windows)
    product = lax.dot_general(
        left[pl.program_id(0)], wide[0], (((0,), (0,)), ((), ())), preferred_element_type=jnp.float32
    )
    product = product * stack_scale
    out[0, 0] = product[:, :channels]
    out[1, 0] = product[:, channels:]


VMEM = pl.BlockSpec(memory_space=pltpu.VMEM)
SMEM = pl.BlockSpec(memory_space=pltpu.SMEM)


def whiten_sources(place, sources):
    freqs, rows, channels = sources.shape[3:]
    depth = 32 * rows
    return pl.pallas_call(
        whiten_kernel,
        out_shape=jax.ShapeDtypeStruct((freqs, depth, 2 * channels), jnp.bfloat16),
        in_specs=[SMEM, VMEM],
        out_specs=VMEM,
        compiler_params=pltpu.CompilerParams(vmem_limit_bytes=20 * 1024 * 1024),
    )(place, sources)


def multiply(place, held, other, wide):
    rows, channels = held.shape[2:]
    depth, width = 32 * rows, channels // 2
    return pl.pallas_call(
        multiply_kernel,
        grid=(2,),
        out_shape=jax.ShapeDtypeStruct((2, 2, width, channels), jnp.float32),
        in_specs=[SMEM, VMEM, VMEM, pl.BlockSpec((1, depth, 2 * channels), lambda f: (f, 0, 0))],
        out_specs=pl.BlockSpec((2, 1, width, channels), lambda f: (0, f, 0, 0)),
        scratch_shapes=[pltpu.VMEM((2, depth, width), jnp.bfloat16)],
        compiler_params=pltpu.CompilerParams(vmem_limit_bytes=28 * 1024 * 1024),
    )(place, held, other, wide)


def on_device(spectra):
    windows, _, freqs, channels = spectra.shape
    width = channels // 2
    place = jnp.stack([lax.axis_index(a) for a in ("zl", "core", "y", "x")]).astype(jnp.int32)
    zh = lax.axis_index("zh")
    block = jnp.transpose(spectra, (2, 1, 0, 3)).reshape(freqs, 2 * windows, channels)

    def half_of(b):
        low = jnp.concatenate([b[0, :, :width], b[1, :, :width]], axis=1)
        high = jnp.concatenate([b[0, :, width:], b[1, :, width:]], axis=1)
        return jnp.where(zh == 0, low, high)

    partner = permute(block, lambda zl, core, y, x, zh: (zl, core, y, x, 1 - zh))
    pieces = jnp.stack([half_of(block), half_of(partner)])
    first = gather_four(jnp.stack([block, partner]), False)
    held = jnp.stack([to_column(pieces, c, False) for c in range(2)])
    held, first = lax.optimization_barrier((held, first))
    wide = whiten_sources(place, gather_four(first, True))
    held = jnp.concatenate([held] + [along_column(held, d) for d in (1, 2, 3)])
    other = permute(held, lambda zl, core, y, x, zh: (zl, 1 - core, y, x, zh))

    crossed = multiply(place, held, other, wide)
    return jnp.transpose(crossed, (3, 0, 1, 2))


def solution(mesh):
    fine = Mesh(mesh.devices.reshape(tuple(SIZES.values())), AXES)
    return jax.shard_map(
        on_device,
        mesh=fine,
        in_specs=(P(("y", "x", "zh"), None, None, ("zl", "core")),),
        out_specs=P(("zl", "core"), None, None, ("y", "x", "zh")),
        check_vma=False,
    )
```

time: 120 us -> 109 us (0.908)
  the two profiles are of different devices: /device:TPU:1 before, /device:TPU:35 now
where the time goes in v3:
time: 109 us; the launch traced here: 108 us
  waiting for transfers between devices  49.3 us (45%)
  starting transfers between devices  43.2 us (40%)
  Pallas kernels  10.9 us (10%)
  local copies, waits for them, and re-layouts  4.57 us (4%)
    ppermute x7, waiting for transfers between devices, permute(): return lax.ppermute(value, AXES, pairs)  49.3 us
    ppermute x7, starting transfers between devices, permute(): return lax.ppermute(value, AXES, pairs)  34.2 us
    all_to_all x2, starting transfers between devices, gather_four(): lax.all_to_all(copies, ('core', 'y', 'x'), 0, 0, axis_index_groups=groups...  9.02 us
    pallas_call x1, Pallas kernels, multiply(): pl.pallas_call(multiply_kernel, grid=(2,), out_shape=jax.ShapeDtypeStruct...  6.47 us
    pallas_call x1, Pallas kernels, whiten_sources(): pl.pallas_call(whiten_kernel, out_shape=jax.ShapeDtypeStruct((freqs, dept...  4.47 us
    broadcast_in_dim x2, local copies, waits for them, and re-layouts, gather_four(): copies = jnp.broadcast_to(value, (4,) + value.shape)  3.36 us
  transfers between devices with their start and end apart: 9, of which 6 were waited for; matrix products, arithmetic and copies ran while one was open for 0% of the time, Pallas kernels for 4%

profile of v3, /device:TPU:35, one launch (start us, length us, event | category | flops | bytes accessed | tf_op | source)
XLA Modules:
  0.0 108.4 jit_solution(17929114202395202845)
XLA Ops:
  0.0 0.9 copy.2
  0.9 14.5 %collective-permute-start = (bf16[2,48,640]{2,1,0:T(8,128)(2,1)S(1)}, bf16[2,48,640]{2,1,0:T(8,128)(2,1)S(1)}, u32[]{:S(2)}, u32[]{:S(2)}) collective-permute-start(bf16[2,48,640]{2,1,0:T(8,128)(2,1)S(1)} %bitcast.11), channel_id=1, source_target_pairs={{0,1},{1,0},{2,3},{3,2},{4,5},{5,4},{6,7},{7,6},{8,9},{9,8},{10,11... | collective-permute-start | bytes 368648 | tf_op jit(solution)/shard_map/ppermute | solution.py:34
  15.5 10.9 %collective-permute-done = bf16[2,48,640]{2,1,0:T(8,128)(2,1)S(1)} collective-permute-done((bf16[2,48,640]{2,1,0:T(8,128)(2,1)S(1)}, bf16[2,48,640]{2,1,0:T(8,128)(2,1)S(1)}, u32[]{:S(2)}, u32[]{:S(2)}) %collective-permute-start) | collective-permute-done | bytes 122912 | tf_op jit(solution)/shard_map/ppermute | solution.py:34
  26.4 1.0 broadcast_in_dim.6
  27.5 4.2 %all-to-all-start = ((bf16[4,2,2,48,640]{4,3,2,1,0:T(8,128)(2,1)}), bf16[4,2,2,48,640]{4,3,2,1,0:T(8,128)(2,1)S(1)}, u32[]{:S(2)}, u32[]{:S(2)}) async-start(bf16[4,2,2,48,640]{4,3,2,1,0:T(8,128)(2,1)} %broadcast_in_dim.6), calls=%async_computation | async-start | bytes 1966080 | tf_op jit(solution)/shard_map/all_to_all | solution.py:45
  31.6 0.1 fusion
  31.7 0.1 fusion.1
  31.8 0.1 maximum_select_fusion
  32.0 7.0 %collective-permute-start.1 = (bf16[2,48,640]{2,1,0:T(8,128)(2,1)S(1)}, bf16[2,48,640]{2,1,0:T(8,128)(2,1)S(1)}, u32[]{:S(2)}, u32[]{:S(2)}) collective-permute-start(bf16[2,48,640]{2,1,0:T(8,128)(2,1)S(1)} %pad_maximum_fusion.2), channel_id=1, source_target_pairs={{0,0},{1,1},{2,256},{3,257},{4,32},{5,33},{6,288},{7,289},{8,64},{... | collective-permute-start | bytes 368648 | tf_op jit(solution)/shard_map/ppermute | solution.py:34
  39.0 1.9 %collective-permute-start.2 = (bf16[2,48,640]{2,1,0:T(8,128)(2,1)S(1)}, bf16[2,48,640]{2,1,0:T(8,128)(2,1)S(1)}, u32[]{:S(2)}, u32[]{:S(2)}) collective-permute-start(bf16[2,48,640]{2,1,0:T(8,128)(2,1)S(1)} %pad_maximum_fusion.2), channel_id=1, source_target_pairs={{0,256},{1,257},{2,0},{3,1},{4,288},{5,289},{6,32},{7,33},{8,320},... | collective-permute-start | bytes 368648 | tf_op jit(solution)/shard_map/ppermute | solution.py:34
  40.9 3.3 %collective-permute-done.1 = bf16[2,48,640]{2,1,0:T(8,128)(2,1)S(1)} collective-permute-done((bf16[2,48,640]{2,1,0:T(8,128)(2,1)S(1)}, bf16[2,48,640]{2,1,0:T(8,128)(2,1)S(1)}, u32[]{:S(2)}, u32[]{:S(2)}) %collective-permute-start.1) | collective-permute-done | bytes 122912 | tf_op jit(solution)/shard_map/ppermute | solution.py:34
  44.2 15.1 %collective-permute-done.2 = bf16[2,48,640]{2,1,0:T(8,128)(2,1)S(1)} collective-permute-done((bf16[2,48,640]{2,1,0:T(8,128)(2,1)S(1)}, bf16[2,48,640]{2,1,0:T(8,128)(2,1)S(1)}, u32[]{:S(2)}, u32[]{:S(2)}) %collective-permute-start.2) | collective-permute-done | bytes 122912 | tf_op jit(solution)/shard_map/ppermute | solution.py:34
  59.3 0.0 all-to-all-done
  59.4 2.3 %broadcast_in_dim.7 = bf16[4,4,2,2,48,640]{5,4,3,2,1,0:T(8,128)(2,1)} broadcast(bf16[4,2,2,48,640]{4,3,2,1,0:T(8,128)(2,1)S(1)} %all-to-all-done), dimensions={1,2,3,4,5} | broadcast | bytes 4915200 | tf_op jit(solution)/shard_map/broadcast_in_dim | solution.py:44
  61.7 4.8 %all-to-all-start.1 = ((bf16[4,4,2,2,48,640]{5,4,3,2,1,0:T(8,128)(2,1)}), bf16[4,4,2,2,48,640]{5,4,3,2,1,0:T(8,128)(2,1)}, u32[]{:S(2)}, u32[]{:S(2)}) async-start(bf16[4,4,2,2,48,640]{5,4,3,2,1,0:T(8,128)(2,1)} %broadcast_in_dim.7), calls=%async_computation.1 | async-start | bytes 7864320 | tf_op jit(solution)/shard_map/all_to_all | solution.py:45
  66.5 1.9 %collective-permute-start.3 = (bf16[2,2,48,640]{3,2,1,0:T(8,128)(2,1)S(1)}, bf16[2,2,48,640]{3,2,1,0:T(8,128)(2,1)S(1)}, u32[]{:S(2)}, u32[]{:S(2)}) collective-permute-start(bf16[2,2,48,640]{3,2,1,0:T(8,128)(2,1)S(1)} %pad_maximum_fusion), channel_id=1, source_target_pairs={{0,64},{1,65},{2,66},{3,67},{4,68},{5,69},{6,70},{7,71},{8,72},{9,... | collective-permute-start | bytes 737288 | tf_op jit(solution)/shard_map/ppermute | solution.py:34
  68.5 1.9 %collective-permute-start.4 = (bf16[2,2,48,640]{3,2,1,0:T(8,128)(2,1)S(1)}, bf16[2,2,48,640]{3,2,1,0:T(8,128)(2,1)S(1)}, u32[]{:S(2)}, u32[]{:S(2)}) collective-permute-start(bf16[2,2,48,640]{3,2,1,0:T(8,128)(2,1)S(1)} %pad_maximum_fusion), channel_id=1, source_target_pairs={{0,128},{1,129},{2,130},{3,131},{4,132},{5,133},{6,134},{7,135},{8... | collective-permute-start | bytes 737288 | tf_op jit(solution)/shard_map/ppermute | solution.py:34
  70.4 4.5 %collective-permute-start.5 = (bf16[2,2,48,640]{3,2,1,0:T(8,128)(2,1)S(1)}, bf16[2,2,48,640]{3,2,1,0:T(8,128)(2,1)S(1)}, u32[]{:S(2)}, u32[]{:S(2)}) collective-permute-start(bf16[2,2,48,640]{3,2,1,0:T(8,128)(2,1)S(1)} %pad_maximum_fusion), channel_id=1, source_target_pairs={{0,192},{1,193},{2,194},{3,195},{4,196},{5,197},{6,198},{7,199},{8... | collective-permute-start | bytes 737288 | tf_op jit(solution)/shard_map/ppermute | solution.py:34
  75.0 0.8 collective-permute-done.3
  75.8 2.8 %collective-permute-done.4 = bf16[2,2,48,640]{3,2,1,0:T(8,128)(2,1)S(1)} collective-permute-done((bf16[2,2,48,640]{3,2,1,0:T(8,128)(2,1)S(1)}, bf16[2,2,48,640]{3,2,1,0:T(8,128)(2,1)S(1)}, u32[]{:S(2)}, u32[]{:S(2)}) %collective-permute-start.4) | collective-permute-done | bytes 245792 | tf_op jit(solution)/shard_map/ppermute | solution.py:34
  78.6 16.3 %collective-permute-done.5 = bf16[2,2,48,640]{3,2,1,0:T(8,128)(2,1)S(1)} collective-permute-done((bf16[2,2,48,640]{3,2,1,0:T(8,128)(2,1)S(1)}, bf16[2,2,48,640]{3,2,1,0:T(8,128)(2,1)S(1)}, u32[]{:S(2)}, u32[]{:S(2)}) %collective-permute-start.5) | collective-permute-done | bytes 245792 | tf_op jit(solution)/shard_map/ppermute | solution.py:34
  95.0 2.4 %collective-permute-start.6 = (bf16[8,2,48,640]{3,2,1,0:T(8,128)(2,1)S(1)}, bf16[8,2,48,640]{3,2,1,0:T(8,128)(2,1)S(1)}, u32[]{:S(2)}, u32[]{:S(2)}) collective-permute-start(bf16[8,2,48,640]{3,2,1,0:T(8,128)(2,1)S(1)} %constant_dynamic-update-slice_fusion.held), channel_id=1, source_target_pairs={{0,32},{1,33},{2,34},{3,35},{4,36},{5,37},{6,38},{7,39},{8,40},{9,... | collective-permute-start | bytes 2949128 | tf_op jit(solution)/shard_map/ppermute | solution.py:34
  97.4 0.1 pad_add_fusion.place
  97.5 0.0 all-to-all-done.1.refs_0_
  97.5 4.5 %shard_map.17.wide = bf16[2,1536,1280]{2,1,0:T(8,128)(2,1)S(1)} custom-call(s32[4]{0:T(128)S(1)} %pad_add_fusion.place, bf16[4,4,2,2,48,640]{5,4,3,2,1,0:T(8,128)(2,1)} %all-to-all-done.1.refs_0_), custom_call_target="tpu_custom_call" | custom-call | tf_op jit(solution)/shard_map/pallas_call | solution.py:158
  101.9 0.0 collective-permute-done.6.other
  102.0 6.5 %shard_map.18 = f32[2,2,320,640]{3,2,1,0:T(8,128)} custom-call(s32[4]{0:T(128)S(1)} %pad_add_fusion.place, bf16[8,2,48,640]{3,2,1,0:T(8,128)(2,1)S(1)} %constant_dynamic-update-slice_fusion.held, bf16[8,2,48,640]{3,2,1,0:T(8,128)(2,1)S(1)} %collective-permute-done.6.other, bf16[2,1536,1280]{2,1,0:T(8,128)(2,1)S(1)} %shard_map.17.wide), custom_call_target="tpu_custom_call" | custom-call | tf_op jit(solution)/shard_map/pallas_call | solution.py:170
  (7 shorter events, 0.2 us)
Async XLA Ops:
  0.9 25.5 %collective-permute-start = (bf16[2,48,640]{2,1,0:T(8,128)(2,1)S(1)}, bf16[2,48,640]{2,1,0:T(8,128)(2,1)S(1)}, u32[]{:S(2)}, u32[]{:S(2)}) collective-permute-start(bf16[2,48,640]{2,1,0:T(8,128)(2,1)S(1)} %bitcast.11), channel_id=1, source_target_pairs={{0,1},{1,0},{2,3},{3,2},{4,5},{5,4},{6,7},{7,6},{8,9},{9,8},{10,11... | collective-permute-start | bytes 368648 | tf_op jit(solution)/shard_map/ppermute | solution.py:34
  27.5 31.9 %all-to-all-start = ((bf16[4,2,2,48,640]{4,3,2,1,0:T(8,128)(2,1)}), bf16[4,2,2,48,640]{4,3,2,1,0:T(8,128)(2,1)S(1)}, u32[]{:S(2)}, u32[]{:S(2)}) async-start(bf16[4,2,2,48,640]{4,3,2,1,0:T(8,128)(2,1)} %broadcast_in_dim.6), calls=%async_computation | async-start | bytes 1966080 | tf_op jit(solution)/shard_map/all_to_all | solution.py:45
  32.0 12.2 %collective-permute-start.1 = (bf16[2,48,640]{2,1,0:T(8,128)(2,1)S(1)}, bf16[2,48,640]{2,1,0:T(8,128)(2,1)S(1)}, u32[]{:S(2)}, u32[]{:S(2)}) collective-permute-start(bf16[2,48,640]{2,1,0:T(8,128)(2,1)S(1)} %pad_maximum_fusion.2), channel_id=1, source_target_pairs={{0,0},{1,1},{2,256},{3,257},{4,32},{5,33},{6,288},{7,289},{8,64},{... | collective-permute-start | bytes 368648 | tf_op jit(solution)/shard_map/ppermute | solution.py:34
  39.0 20.4 %collective-permute-start.2 = (bf16[2,48,640]{2,1,0:T(8,128)(2,1)S(1)}, bf16[2,48,640]{2,1,0:T(8,128)(2,1)S(1)}, u32[]{:S(2)}, u32[]{:S(2)}) collective-permute-start(bf16[2,48,640]{2,1,0:T(8,128)(2,1)S(1)} %pad_maximum_fusion.2), channel_id=1, source_target_pairs={{0,256},{1,257},{2,0},{3,1},{4,288},{5,289},{6,32},{7,33},{8,320},... | collective-permute-start | bytes 368648 | tf_op jit(solution)/shard_map/ppermute | solution.py:34
  61.7 35.8 %all-to-all-start.1 = ((bf16[4,4,2,2,48,640]{5,4,3,2,1,0:T(8,128)(2,1)}), bf16[4,4,2,2,48,640]{5,4,3,2,1,0:T(8,128)(2,1)}, u32[]{:S(2)}, u32[]{:S(2)}) async-start(bf16[4,4,2,2,48,640]{5,4,3,2,1,0:T(8,128)(2,1)} %broadcast_in_dim.7), calls=%async_computation.1 | async-start | bytes 7864320 | tf_op jit(solution)/shard_map/all_to_all | solution.py:45
  66.5 9.2 %collective-permute-start.3 = (bf16[2,2,48,640]{3,2,1,0:T(8,128)(2,1)S(1)}, bf16[2,2,48,640]{3,2,1,0:T(8,128)(2,1)S(1)}, u32[]{:S(2)}, u32[]{:S(2)}) collective-permute-start(bf16[2,2,48,640]{3,2,1,0:T(8,128)(2,1)S(1)} %pad_maximum_fusion), channel_id=1, source_target_pairs={{0,64},{1,65},{2,66},{3,67},{4,68},{5,69},{6,70},{7,71},{8,72},{9,... | collective-permute-start | bytes 737288 | tf_op jit(solution)/shard_map/ppermute | solution.py:34
  68.5 10.1 %collective-permute-start.4 = (bf16[2,2,48,640]{3,2,1,0:T(8,128)(2,1)S(1)}, bf16[2,2,48,640]{3,2,1,0:T(8,128)(2,1)S(1)}, u32[]{:S(2)}, u32[]{:S(2)}) collective-permute-start(bf16[2,2,48,640]{3,2,1,0:T(8,128)(2,1)S(1)} %pad_maximum_fusion), channel_id=1, source_target_pairs={{0,128},{1,129},{2,130},{3,131},{4,132},{5,133},{6,134},{7,135},{8... | collective-permute-start | bytes 737288 | tf_op jit(solution)/shard_map/ppermute | solution.py:34
  70.4 24.5 %collective-permute-start.5 = (bf16[2,2,48,640]{3,2,1,0:T(8,128)(2,1)S(1)}, bf16[2,2,48,640]{3,2,1,0:T(8,128)(2,1)S(1)}, u32[]{:S(2)}, u32[]{:S(2)}) collective-permute-start(bf16[2,2,48,640]{3,2,1,0:T(8,128)(2,1)S(1)} %pad_maximum_fusion), channel_id=1, source_target_pairs={{0,192},{1,193},{2,194},{3,195},{4,196},{5,197},{6,198},{7,199},{8... | collective-permute-start | bytes 737288 | tf_op jit(solution)/shard_map/ppermute | solution.py:34
  95.0 7.0 %collective-permute-start.6 = (bf16[8,2,48,640]{3,2,1,0:T(8,128)(2,1)S(1)}, bf16[8,2,48,640]{3,2,1,0:T(8,128)(2,1)S(1)}, u32[]{:S(2)}, u32[]{:S(2)}) collective-permute-start(bf16[8,2,48,640]{3,2,1,0:T(8,128)(2,1)S(1)} %constant_dynamic-update-slice_fusion.held), channel_id=1, source_target_pairs={{0,32},{1,33},{2,34},{3,35},{4,36},{5,37},{6,38},{7,39},{8,40},{9,... | collective-permute-start | bytes 2949128 | tf_op jit(solution)/shard_map/ppermute | solution.py:34

commit v4 on v3

--- a/solution.py
+++ b/solution.py
@@ -34,15 +34,9 @@
     return lax.ppermute(value, AXES, pairs)
 
 
-def groups_of(swapped):
-    along_x = [[[c * 16 + y * 4 + x for x in range(4)] for y in range(4)] for c in range(2)]
-    along_y = [[[c * 16 + y * 4 + x for y in range(4)] for x in range(4)] for c in range(2)]
-    return along_y[0] + along_x[1] if swapped else along_x[0] + along_y[1]
-
-
-def gather_four(value, swapped):
-    copies = jnp.broadcast_to(value, (4,) + value.shape)
-    return lax.all_to_all(copies, ("core", "y", "x"), 0, 0, axis_index_groups=groups_of(swapped))
+def gather_plane(block):
+    copies = jnp.broadcast_to(block, (16,) + block.shape)
+    return lax.all_to_all(copies, ("y", "x"), 0, 0)
 
 
 def to_column(value, copy, cross):
@@ -78,28 +72,26 @@
 
 
 def whiten_kernel(place, *refs):
-    sources, wide = refs
-    core = place[1]
-    freqs, rows, channels = sources.shape[3:]
+    sources, wide = refs[:2], refs[2]
+    freqs, rows, channels = sources[0].shape[1:]
     windows = 16 * rows
     for f in range(freqs):
 
-        def add(second, total):
-            for first in range(4):
-                for zr in range(2):
-                    total = total + fold(energy_of(sources[second, first, zr, f])[2])
+        def add(a, total):
+            for i in range(4):
+                for ref in sources:
+                    total = total + fold(energy_of(ref[a * 4 + i, f])[2])
             return total
 
         floor = floor_of(lax.fori_loop(0, 4, add, jnp.zeros((8, channels), jnp.float32)), windows)
 
-        def whiten(second, carry):
-            for first in range(4):
-                g = jnp.where(core == 0, second * 4 + first, first * 4 + second)
-                for zr in range(2):
-                    real, imag, energy = energy_of(sources[second, first, zr, f])
+        def whiten(a, carry):
+            for i in range(4):
+                for zr, ref in enumerate(sources):
+                    real, imag, energy = energy_of(ref[a * 4 + i, f])
                     scale = lax.rsqrt(energy + floor)
                     real, imag = real * scale, imag * scale
-                    row = pl.multiple_of((zr * 16 + g) * rows, rows)
+                    row = pl.multiple_of((zr * 16 + a * 4 + i) * rows, rows)
                     wide[f, pl.ds(row, rows), :channels] = stacked(real, imag)
                     wide[f, pl.ds(row, rows), channels:] = stacked(imag, -real)
             return carry
@@ -153,15 +145,16 @@
 
 
 def whiten_sources(place, sources):
-    freqs, rows, channels = sources.shape[3:]
+    freqs, rows, channels = sources[0].shape[1:]
     depth = 32 * rows
     return pl.pallas_call(
         whiten_kernel,
         out_shape=jax.ShapeDtypeStruct((freqs, depth, 2 * channels), jnp.bfloat16),
-        in_specs=[SMEM, VMEM],
+        in_specs=[SMEM] + [VMEM] * 2,
         out_specs=VMEM,
         compiler_params=pltpu.CompilerParams(vmem_limit_bytes=20 * 1024 * 1024),
-    )(place, sources)
+        cost_estimate=pl.CostEstimate(flops=20 * depth * channels, bytes_accessed=8 * depth * channels, transcendentals=depth * channels),
+    )(place, *sources)
 
 
 def multiply(place, held, other, wide):
@@ -192,10 +185,10 @@
 
     partner = permute(block, lambda zl, core, y, x, zh: (zl, core, y, x, 1 - zh))
     pieces = jnp.stack([half_of(block), half_of(partner)])
-    first = gather_four(jnp.stack([block, partner]), False)
+    near = gather_plane(block)
     held = jnp.stack([to_column(pieces, c, False) for c in range(2)])
-    held, first = lax.optimization_barrier((held, first))
-    wide = whiten_sources(place, gather_four(first, True))
+    partner, near = lax.optimization_barrier((partner, near))
+    wide = whiten_sources(place, [near, gather_plane(partner)])
     held = jnp.concatenate([held] + [along_column(held, d) for d in (1, 2, 3)])
     other = permute(held, lambda zl, core, y, x, zh: (zl, 1 - core, y, x, zh))
 

time: 109 us -> 104 us (0.954)
  the two profiles are of different devices: /device:TPU:35 before, /device:TPU:1 now
where the time goes in v4:
time: 104 us; the launch traced here: 103 us
  starting transfers between devices  67.1 us (65%)
  waiting for transfers between devices  20.6 us (20%)
  Pallas kernels  11 us (11%)
  local copies, waits for them, and re-layouts  4.07 us (4%)
    ppermute x7, starting transfers between devices, permute(): return lax.ppermute(value, AXES, pairs)  46.2 us
    all_to_all x2, starting transfers between devices, gather_plane(): return lax.all_to_all(copies, ('y', 'x'), 0, 0)  20.9 us
    ppermute x7, waiting for transfers between devices, permute(): return lax.ppermute(value, AXES, pairs)  17.9 us
    pallas_call x1, Pallas kernels, multiply(): pl.pallas_call(multiply_kernel, grid=(2,), out_shape=jax.ShapeDtypeStruct...  7.13 us
    pallas_call x1, Pallas kernels, whiten_sources(): pl.pallas_call(whiten_kernel, out_shape=jax.ShapeDtypeStruct((freqs, dept...  3.9 us
    broadcast_in_dim x2, local copies, waits for them, and re-layouts, gather_plane(): copies = jnp.broadcast_to(block, (16,) + block.shape)  2.85 us
    all_to_all x2, waiting for transfers between devices, gather_plane(): return lax.all_to_all(copies, ('y', 'x'), 0, 0)  2.62 us
  transfers between devices with their start and end apart: 9, of which 4 were waited for; matrix products, arithmetic and copies ran while one was open for 2% of the time, Pallas kernels for 4%

profile of v4, /device:TPU:1, one launch (start us, length us, event | category | flops | bytes accessed | tf_op | source)
XLA Modules:
  0.0 103.2 jit_solution(10297816792175830864)
XLA Ops:
  0.0 0.9 copy.2
  0.9 1.4 %broadcast_in_dim.6 = bf16[16,2,48,640]{3,2,1,0:T(8,128)(2,1)} broadcast(bf16[2,48,640]{2,1,0:T(8,128)(2,1)S(1)} %bitcast.11), dimensions={1,2,3} | broadcast | bytes 2088960 | tf_op jit(solution)/shard_map/broadcast_in_dim | solution.py:38
  2.3 7.6 %all-to-all-start = ((bf16[16,2,48,640]{3,2,1,0:T(8,128)(2,1)}), bf16[16,2,48,640]{3,2,1,0:T(8,128)(2,1)S(1)}, u32[]{:S(2)}, u32[]{:S(2)}) async-start(bf16[16,2,48,640]{3,2,1,0:T(8,128)(2,1)} %broadcast_in_dim.6), calls=%async_computation | async-start | bytes 3932160 | tf_op jit(solution)/shard_map/all_to_all | solution.py:39
  9.9 15.4 %collective-permute-start = (bf16[2,48,640]{2,1,0:T(8,128)(2,1)S(1)}, bf16[2,48,640]{2,1,0:T(8,128)(2,1)S(1)}, u32[]{:S(2)}, u32[]{:S(2)}) collective-permute-start(bf16[2,48,640]{2,1,0:T(8,128)(2,1)S(1)} %bitcast.12), channel_id=1, source_target_pairs={{0,1},{1,0},{2,3},{3,2},{4,5},{5,4},{6,7},{7,6},{8,9},{9,8},{10,11... | collective-permute-start | bytes 368648 | tf_op jit(solution)/shard_map/ppermute | solution.py:34
  25.4 0.1 fusion
  25.5 2.6 %collective-permute-done = bf16[2,48,640]{2,1,0:T(8,128)(2,1)S(1)} collective-permute-done((bf16[2,48,640]{2,1,0:T(8,128)(2,1)S(1)}, bf16[2,48,640]{2,1,0:T(8,128)(2,1)S(1)}, u32[]{:S(2)}, u32[]{:S(2)}) %collective-permute-start) | collective-permute-done | bytes 122912 | tf_op jit(solution)/shard_map/ppermute | solution.py:34
  28.1 0.1 fusion.1
  28.2 0.1 maximum_select_fusion
  28.4 14.4 %collective-permute-start.2 = (bf16[2,48,640]{2,1,0:T(8,128)(2,1)S(1)}, bf16[2,48,640]{2,1,0:T(8,128)(2,1)S(1)}, u32[]{:S(2)}, u32[]{:S(2)}) collective-permute-start(bf16[2,48,640]{2,1,0:T(8,128)(2,1)S(1)} %pad_maximum_fusion.1), channel_id=1, source_target_pairs={{0,256},{1,257},{2,0},{3,1},{4,288},{5,289},{6,32},{7,33},{8,320},... | collective-permute-start | bytes 368648 | tf_op jit(solution)/shard_map/ppermute | solution.py:34
  42.8 1.9 %collective-permute-start.1 = (bf16[2,48,640]{2,1,0:T(8,128)(2,1)S(1)}, bf16[2,48,640]{2,1,0:T(8,128)(2,1)S(1)}, u32[]{:S(2)}, u32[]{:S(2)}) collective-permute-start(bf16[2,48,640]{2,1,0:T(8,128)(2,1)S(1)} %pad_maximum_fusion.1), channel_id=1, source_target_pairs={{0,0},{1,1},{2,256},{3,257},{4,32},{5,33},{6,288},{7,289},{8,64},{... | collective-permute-start | bytes 368648 | tf_op jit(solution)/shard_map/ppermute | solution.py:34
  44.7 0.0 all-to-all-done.refs_0_
  44.7 1.4 %broadcast_in_dim.7 = bf16[16,2,48,640]{3,2,1,0:T(8,128)(2,1)} broadcast(bf16[2,48,640]{2,1,0:T(8,128)(2,1)S(1)} %collective-permute-done), dimensions={1,2,3} | broadcast | bytes 2088960 | tf_op jit(solution)/shard_map/broadcast_in_dim | solution.py:38
  46.2 13.3 %all-to-all-start.1 = ((bf16[16,2,48,640]{3,2,1,0:T(8,128)(2,1)}), bf16[16,2,48,640]{3,2,1,0:T(8,128)(2,1)}, u32[]{:S(2)}, u32[]{:S(2)}) async-start(bf16[16,2,48,640]{3,2,1,0:T(8,128)(2,1)} %broadcast_in_dim.7), calls=%async_computation.1 | async-start | bytes 3932160 | tf_op jit(solution)/shard_map/all_to_all | solution.py:39
  59.5 0.0 collective-permute-done.2
  59.5 0.0 collective-permute-done.1
  59.5 1.9 %collective-permute-start.5 = (bf16[2,2,48,640]{3,2,1,0:T(8,128)(2,1)S(1)}, bf16[2,2,48,640]{3,2,1,0:T(8,128)(2,1)S(1)}, u32[]{:S(2)}, u32[]{:S(2)}) collective-permute-start(bf16[2,2,48,640]{3,2,1,0:T(8,128)(2,1)S(1)} %pad_maximum_fusion), channel_id=1, source_target_pairs={{0,192},{1,193},{2,194},{3,195},{4,196},{5,197},{6,198},{7,199},{8... | collective-permute-start | bytes 737288 | tf_op jit(solution)/shard_map/ppermute | solution.py:34
  61.5 8.1 %collective-permute-start.4 = (bf16[2,2,48,640]{3,2,1,0:T(8,128)(2,1)S(1)}, bf16[2,2,48,640]{3,2,1,0:T(8,128)(2,1)S(1)}, u32[]{:S(2)}, u32[]{:S(2)}) collective-permute-start(bf16[2,2,48,640]{3,2,1,0:T(8,128)(2,1)S(1)} %pad_maximum_fusion), channel_id=1, source_target_pairs={{0,128},{1,129},{2,130},{3,131},{4,132},{5,133},{6,134},{7,135},{8... | collective-permute-start | bytes 737288 | tf_op jit(solution)/shard_map/ppermute | solution.py:34
  69.6 1.9 %collective-permute-start.3 = (bf16[2,2,48,640]{3,2,1,0:T(8,128)(2,1)S(1)}, bf16[2,2,48,640]{3,2,1,0:T(8,128)(2,1)S(1)}, u32[]{:S(2)}, u32[]{:S(2)}) collective-permute-start(bf16[2,2,48,640]{3,2,1,0:T(8,128)(2,1)S(1)} %pad_maximum_fusion), channel_id=1, source_target_pairs={{0,64},{1,65},{2,66},{3,67},{4,68},{5,69},{6,70},{7,71},{8,72},{9,... | collective-permute-start | bytes 737288 | tf_op jit(solution)/shard_map/ppermute | solution.py:34
  71.6 7.9 %collective-permute-done.3 = bf16[2,2,48,640]{3,2,1,0:T(8,128)(2,1)S(1)} collective-permute-done((bf16[2,2,48,640]{3,2,1,0:T(8,128)(2,1)S(1)}, bf16[2,2,48,640]{3,2,1,0:T(8,128)(2,1)S(1)}, u32[]{:S(2)}, u32[]{:S(2)}) %collective-permute-start.3) | collective-permute-done | bytes 245792 | tf_op jit(solution)/shard_map/ppermute | solution.py:34
  79.5 7.4 %collective-permute-done.4 = bf16[2,2,48,640]{3,2,1,0:T(8,128)(2,1)S(1)} collective-permute-done((bf16[2,2,48,640]{3,2,1,0:T(8,128)(2,1)S(1)}, bf16[2,2,48,640]{3,2,1,0:T(8,128)(2,1)S(1)}, u32[]{:S(2)}, u32[]{:S(2)}) %collective-permute-start.4) | collective-permute-done | bytes 245792 | tf_op jit(solution)/shard_map/ppermute | solution.py:34
  87.0 0.0 collective-permute-done.5
  87.0 2.4 %collective-permute-start.6 = (bf16[8,2,48,640]{3,2,1,0:T(8,128)(2,1)S(1)}, bf16[8,2,48,640]{3,2,1,0:T(8,128)(2,1)}, u32[]{:S(2)}, u32[]{:S(2)}) collective-permute-start(bf16[8,2,48,640]{3,2,1,0:T(8,128)(2,1)S(1)} %constant_dynamic-update-slice_fusion.held), channel_id=1, source_target_pairs={{0,32},{1,33},{2,34},{3,35},{4,36},{5,37},{6,38},{7,39},{8,40},{9,... | collective-permute-start | bytes 2949128 | tf_op jit(solution)/shard_map/ppermute | solution.py:34
  89.4 0.1 pad_add_fusion.place
  89.5 2.6 %all-to-all-done.1.refs_1_ = bf16[16,2,48,640]{3,2,1,0:T(8,128)(2,1)} async-done(((bf16[16,2,48,640]{3,2,1,0:T(8,128)(2,1)}), bf16[16,2,48,640]{3,2,1,0:T(8,128)(2,1)}, u32[]{:S(2)}, u32[]{:S(2)}) %all-to-all-start.1) | async-done | bytes 1966112 | tf_op jit(solution)/shard_map/all_to_all | solution.py:39
  92.1 3.9 %shard_map.17.wide = bf16[2,1536,1280]{2,1,0:T(8,128)(2,1)S(1)} custom-call(s32[4]{0:T(128)S(1)} %pad_add_fusion.place, bf16[16,2,48,640]{3,2,1,0:T(8,128)(2,1)S(1)} %all-to-all-done.refs_0_, bf16[16,2,48,640]{3,2,1,0:T(8,128)(2,1)} %all-to-all-done.1.refs_1_), custom_call_target="tpu_custom_call" | custom-call | flops 19660800 | bytes 7864320 | tf_op jit(solution)/shard_map/pallas_call | solution.py:150
  96.0 0.0 collective-permute-done.6.other
  96.0 7.1 %shard_map.18 = f32[2,2,320,640]{3,2,1,0:T(8,128)} custom-call(s32[4]{0:T(128)S(1)} %pad_add_fusion.place, bf16[8,2,48,640]{3,2,1,0:T(8,128)(2,1)S(1)} %constant_dynamic-update-slice_fusion.held, bf16[8,2,48,640]{3,2,1,0:T(8,128)(2,1)} %collective-permute-done.6.other, bf16[2,1536,1280]{2,1,0:T(8,128)(2,1)S(1)} %shard_map.17.wide), custom_call_target="tpu_custom_call" | custom-call | tf_op jit(solution)/shard_map/pallas_call | solution.py:163
  (7 shorter events, 0.2 us)
Async XLA Ops:
  2.3 42.4 %all-to-all-start = ((bf16[16,2,48,640]{3,2,1,0:T(8,128)(2,1)}), bf16[16,2,48,640]{3,2,1,0:T(8,128)(2,1)S(1)}, u32[]{:S(2)}, u32[]{:S(2)}) async-start(bf16[16,2,48,640]{3,2,1,0:T(8,128)(2,1)} %broadcast_in_dim.6), calls=%async_computation | async-start | bytes 3932160 | tf_op jit(solution)/shard_map/all_to_all | solution.py:39
  9.9 18.2 %collective-permute-start = (bf16[2,48,640]{2,1,0:T(8,128)(2,1)S(1)}, bf16[2,48,640]{2,1,0:T(8,128)(2,1)S(1)}, u32[]{:S(2)}, u32[]{:S(2)}) collective-permute-start(bf16[2,48,640]{2,1,0:T(8,128)(2,1)S(1)} %bitcast.12), channel_id=1, source_target_pairs={{0,1},{1,0},{2,3},{3,2},{4,5},{5,4},{6,7},{7,6},{8,9},{9,8},{10,11... | collective-permute-start | bytes 368648 | tf_op jit(solution)/shard_map/ppermute | solution.py:34
  28.4 31.1 %collective-permute-start.2 = (bf16[2,48,640]{2,1,0:T(8,128)(2,1)S(1)}, bf16[2,48,640]{2,1,0:T(8,128)(2,1)S(1)}, u32[]{:S(2)}, u32[]{:S(2)}) collective-permute-start(bf16[2,48,640]{2,1,0:T(8,128)(2,1)S(1)} %pad_maximum_fusion.1), channel_id=1, source_target_pairs={{0,256},{1,257},{2,0},{3,1},{4,288},{5,289},{6,32},{7,33},{8,320},... | collective-permute-start | bytes 368648 | tf_op jit(solution)/shard_map/ppermute | solution.py:34
  42.8 16.7 %collective-permute-start.1 = (bf16[2,48,640]{2,1,0:T(8,128)(2,1)S(1)}, bf16[2,48,640]{2,1,0:T(8,128)(2,1)S(1)}, u32[]{:S(2)}, u32[]{:S(2)}) collective-permute-start(bf16[2,48,640]{2,1,0:T(8,128)(2,1)S(1)} %pad_maximum_fusion.1), channel_id=1, source_target_pairs={{0,0},{1,1},{2,256},{3,257},{4,32},{5,33},{6,288},{7,289},{8,64},{... | collective-permute-start | bytes 368648 | tf_op jit(solution)/shard_map/ppermute | solution.py:34
  46.2 45.9 %all-to-all-start.1 = ((bf16[16,2,48,640]{3,2,1,0:T(8,128)(2,1)}), bf16[16,2,48,640]{3,2,1,0:T(8,128)(2,1)}, u32[]{:S(2)}, u32[]{:S(2)}) async-start(bf16[16,2,48,640]{3,2,1,0:T(8,128)(2,1)} %broadcast_in_dim.7), calls=%async_computation.1 | async-start | bytes 3932160 | tf_op jit(solution)/shard_map/all_to_all | solution.py:39
  59.5 27.4 %collective-permute-start.5 = (bf16[2,2,48,640]{3,2,1,0:T(8,128)(2,1)S(1)}, bf16[2,2,48,640]{3,2,1,0:T(8,128)(2,1)S(1)}, u32[]{:S(2)}, u32[]{:S(2)}) collective-permute-start(bf16[2,2,48,640]{3,2,1,0:T(8,128)(2,1)S(1)} %pad_maximum_fusion), channel_id=1, source_target_pairs={{0,192},{1,193},{2,194},{3,195},{4,196},{5,197},{6,198},{7,199},{8... | collective-permute-start | bytes 737288 | tf_op jit(solution)/shard_map/ppermute | solution.py:34
  61.5 25.5 %collective-permute-start.4 = (bf16[2,2,48,640]{3,2,1,0:T(8,128)(2,1)S(1)}, bf16[2,2,48,640]{3,2,1,0:T(8,128)(2,1)S(1)}, u32[]{:S(2)}, u32[]{:S(2)}) collective-permute-start(bf16[2,2,48,640]{3,2,1,0:T(8,128)(2,1)S(1)} %pad_maximum_fusion), channel_id=1, source_target_pairs={{0,128},{1,129},{2,130},{3,131},{4,132},{5,133},{6,134},{7,135},{8... | collective-permute-start | bytes 737288 | tf_op jit(solution)/shard_map/ppermute | solution.py:34
  69.6 9.9 %collective-permute-start.3 = (bf16[2,2,48,640]{3,2,1,0:T(8,128)(2,1)S(1)}, bf16[2,2,48,640]{3,2,1,0:T(8,128)(2,1)S(1)}, u32[]{:S(2)}, u32[]{:S(2)}) collective-permute-start(bf16[2,2,48,640]{3,2,1,0:T(8,128)(2,1)S(1)} %pad_maximum_fusion), channel_id=1, source_target_pairs={{0,64},{1,65},{2,66},{3,67},{4,68},{5,69},{6,70},{7,71},{8,72},{9,... | collective-permute-start | bytes 737288 | tf_op jit(solution)/shard_map/ppermute | solution.py:34
  87.0 9.0 %collective-permute-start.6 = (bf16[8,2,48,640]{3,2,1,0:T(8,128)(2,1)S(1)}, bf16[8,2,48,640]{3,2,1,0:T(8,128)(2,1)}, u32[]{:S(2)}, u32[]{:S(2)}) collective-permute-start(bf16[8,2,48,640]{3,2,1,0:T(8,128)(2,1)S(1)} %constant_dynamic-update-slice_fusion.held), channel_id=1, source_target_pairs={{0,32},{1,33},{2,34},{3,35},{4,36},{5,37},{6,38},{7,39},{8,40},{9,... | collective-permute-start | bytes 2949128 | tf_op jit(solution)/shard_map/ppermute | solution.py:34

commit v5 on v4

--- a/solution.py
+++ b/solution.py
@@ -42,7 +42,7 @@
 def to_column(value, copy, cross):
     def target(zl, core, y, x, zh):
         s, g = zl * 2 + core, y * 4 + x
-        group, slot = (g + copy) % 2, g // 2
+        group, slot = ((g ^ s) + copy) % 2, (g ^ s) // 2
         return (group * 4 + slot // 2, slot % 2, s // 4, s % 4, 1 - zh if cross else zh)
 
     return permute(value, target)
@@ -71,19 +71,30 @@
     return jnp.concatenate([upper, lower], axis=0).astype(jnp.bfloat16)
 
 
-def whiten_kernel(place, *refs):
-    sources, wide = refs[:2], refs[2]
+def energy_kernel(blocks, out):
+    freqs, rows, channels = blocks.shape[1:]
+    for f in range(freqs):
+
+        def add(a, total):
+            for i in range(4):
+                total = total + fold(energy_of(blocks[a * 4 + i, f])[2])
+            return total
+
+        out[f] = lax.fori_loop(0, 4, add, jnp.zeros((8, channels), jnp.float32))
+
+
+def whiten_kernel(near, far, energies, wide):
+    sources = (near, far)
     freqs, rows, channels = sources[0].shape[1:]
     windows = 16 * rows
     for f in range(freqs):
 
         def add(a, total):
             for i in range(4):
-                for ref in sources:
-                    total = total + fold(energy_of(ref[a * 4 + i, f])[2])
+                total = total + fold(energy_of(far[a * 4 + i, f])[2])
             return total
 
-        floor = floor_of(lax.fori_loop(0, 4, add, jnp.zeros((8, channels), jnp.float32)), windows)
+        floor = floor_of(lax.fori_loop(0, 4, add, energies[f]), windows)
 
         def whiten(a, carry):
             for i in range(4):
@@ -99,62 +110,75 @@
         lax.fori_loop(0, 4, whiten, 0)
 
 
-def multiply_kernel(place, held, other, wide, out, left):
-    zl, core = place[0], place[1]
+def multiply_kernel(place, held, other, wide, out, left, products, sems):
+    zl, core, column = place[0], place[1], place[2] * 4 + place[3]
     rows, channels = held.shape[2:]
     width = channels // 2
     windows = 16 * rows
 
-    @pl.when(pl.program_id(0) == 0)
-    def _():
-        def add(a, total):
-            for ref in (held, other):
-                for zr in range(2):
-                    total = total + fold(energy_of(ref[a, zr])[2])
-            return total
-
-        floor = floor_of(lax.fori_loop(0, 8, add, jnp.zeros((8, channels), jnp.float32)), windows)
-
-        def whiten(a, carry):
-            along = lax.rem(lax.bitwise_xor(zl, a // 2), 4)
-            copy = lax.rem(zl // 4 + a, 2)
-            for n, ref in enumerate((held, other)):
-                g = along * 4 + lax.bitwise_xor(core, n) * 2 + copy
-                for zr in range(2):
-                    real, imag, energy = energy_of(ref[a, zr])
-                    scale = lax.rsqrt(energy + floor)
-                    row = pl.multiple_of((zr * 16 + g) * rows, rows)
-                    block = stacked(real * scale, imag * scale)
-                    for f in range(2):
-                        left[f, pl.ds(row, rows), :] = block[:, f * width : (f + 1) * width]
-            return carry
-
-        lax.fori_loop(0, 8, whiten, 0)
+    def add(a, total):
+        for ref in (held, other):
+            for zr in range(2):
+                total = total + fold(energy_of(ref[a, zr])[2])
+        return total
+
+    floor = floor_of(lax.fori_loop(0, 8, add, jnp.zeros((8, channels), jnp.float32)), windows)
+
+    def whiten(a, carry):
+        along = lax.rem(lax.bitwise_xor(zl, a // 2), 4)
+        copy = lax.rem(zl // 4 + a, 2)
+        for n, ref in enumerate((held, other)):
+            g = lax.bitwise_xor(along * 4 + lax.bitwise_xor(core, n) * 2 + copy, column)
+            for zr in range(2):
+                real, imag, energy = energy_of(ref[a, zr])
+                scale = lax.rsqrt(energy + floor)
+                row = pl.multiple_of((zr * 16 + g) * rows, rows)
+                block = stacked(real * scale, imag * scale)
+                for f in range(2):
+                    left[f, pl.ds(row, rows), :] = block[:, f * width : (f + 1) * width]
+        return carry
+
+    lax.fori_loop(0, 8, whiten, 0)
 
     stack_scale = 1.0 / math.sqrt(windows)
-    product = lax.dot_general(
-        left[pl.program_id(0)], wide[0], (((0,), (0,)), ((), ())), preferred_element_type=jnp.float32
-    )
-    product = product * stack_scale
-    out[0, 0] = product[:, :channels]
-    out[1, 0] = product[:, channels:]
+    copies = []
+    for f in range(2):
+        product = lax.dot_general(left[f], wide[f], (((0,), (0,)), ((), ())), preferred_element_type=jnp.float32)
+        product = product * stack_scale
+        for part in range(2):
+            products[part, f] = product[:, part * channels : (part + 1) * channels]
+            copy = pltpu.make_async_copy(products.at[part, f], out.at[part, f], sems.at[part, f])
+            copy.start()
+            copies.append(copy)
+    for copy in copies:
+        copy.wait()
 
 
 VMEM = pl.BlockSpec(memory_space=pltpu.VMEM)
 SMEM = pl.BlockSpec(memory_space=pltpu.SMEM)
 
 
-def whiten_sources(place, sources):
-    freqs, rows, channels = sources[0].shape[1:]
+def energies_of(blocks):
+    freqs, rows, channels = blocks.shape[1:]
+    return pl.pallas_call(
+        energy_kernel,
+        out_shape=jax.ShapeDtypeStruct((freqs, 8, channels), jnp.float32),
+        in_specs=[VMEM],
+        out_specs=VMEM,
+        compiler_params=pltpu.CompilerParams(vmem_limit_bytes=8 * 1024 * 1024),
+    )(blocks)
+
+
+def whiten_sources(near, far, energies):
+    freqs, rows, channels = near.shape[1:]
     depth = 32 * rows
     return pl.pallas_call(
         whiten_kernel,
         out_shape=jax.ShapeDtypeStruct((freqs, depth, 2 * channels), jnp.bfloat16),
-        in_specs=[SMEM] + [VMEM] * 2,
+        in_specs=[VMEM] * 3,
         out_specs=VMEM,
         compiler_params=pltpu.CompilerParams(vmem_limit_bytes=20 * 1024 * 1024),
-        cost_estimate=pl.CostEstimate(flops=20 * depth * channels, bytes_accessed=8 * depth * channels, transcendentals=depth * channels),
-    )(place, *sources)
+    )(near, far, energies)
 
 
 def multiply(place, held, other, wide):
@@ -162,12 +186,15 @@
     depth, width = 32 * rows, channels // 2
     return pl.pallas_call(
         multiply_kernel,
-        grid=(2,),
         out_shape=jax.ShapeDtypeStruct((2, 2, width, channels), jnp.float32),
-        in_specs=[SMEM, VMEM, VMEM, pl.BlockSpec((1, depth, 2 * channels), lambda f: (f, 0, 0))],
-        out_specs=pl.BlockSpec((2, 1, width, channels), lambda f: (0, f, 0, 0)),
-        scratch_shapes=[pltpu.VMEM((2, depth, width), jnp.bfloat16)],
-        compiler_params=pltpu.CompilerParams(vmem_limit_bytes=28 * 1024 * 1024),
+        in_specs=[SMEM, VMEM, VMEM, VMEM],
+        out_specs=pl.BlockSpec(memory_space=pl.ANY),
+        scratch_shapes=[
+            pltpu.VMEM((2, depth, width), jnp.bfloat16),
+            pltpu.VMEM((2, 2, width, channels), jnp.float32),
+            pltpu.SemaphoreType.DMA((2, 2)),
+        ],
+        compiler_params=pltpu.CompilerParams(vmem_limit_bytes=20 * 1024 * 1024),
     )(place, held, other, wide)
 
 
@@ -188,7 +215,7 @@
     near = gather_plane(block)
     held = jnp.stack([to_column(pieces, c, False) for c in range(2)])
     partner, near = lax.optimization_barrier((partner, near))
-    wide = whiten_sources(place, [near, gather_plane(partner)])
+    wide = whiten_sources(near, gather_plane(partner), energies_of(near))
     held = jnp.concatenate([held] + [along_column(held, d) for d in (1, 2, 3)])
     other = permute(held, lambda zl, core, y, x, zh: (zl, 1 - core, y, x, zh))
 

time: 104 us -> 99.2 us (0.954)
  starting transfers between devices: 67.1 us -> 62.1 us
  waiting for transfers between devices: 20.6 us -> 21.7 us
    ppermute x7, starting transfers between devices: 46.2 us -> 43.4 us  [permute(): return lax.ppermute(value, AXES, pairs)]
    all_to_all x2, starting transfers between devices: 20.9 us -> 18.6 us  [gather_plane(): return lax.all_to_all(copies, ('y', 'x'), 0, 0)]
    ppermute x7, waiting for transfers between devices: 17.9 us -> 19.7 us  [permute(): return lax.ppermute(value, AXES, pairs)]
    pallas_call x1 -> x2, Pallas kernels: 7.13 us -> 6.95 us  [the longest x1 6.54 us: multiply(): pl.pallas_call(multiply_kernel, out_shape=jax.ShapeDtypeStruct((2, 2, wid...]
where the time goes in v5:
time: 99.2 us; the launch traced here: 98.8 us
  starting transfers between devices  62.1 us (63%)
  waiting for transfers between devices  21.7 us (22%)
  Pallas kernels  10.5 us (11%)
  local copies, waits for them, and re-layouts  4.07 us (4%)
    ppermute x7, starting transfers between devices, permute(): return lax.ppermute(value, AXES, pairs)  43.4 us
    ppermute x7, waiting for transfers between devices, permute(): return lax.ppermute(value, AXES, pairs)  19.7 us
    all_to_all x2, starting transfers between devices, gather_plane(): return lax.all_to_all(copies, ('y', 'x'), 0, 0)  18.6 us
    pallas_call x1, Pallas kernels, multiply(): pl.pallas_call(multiply_kernel, out_shape=jax.ShapeDtypeStruct((2, 2, wid...  6.54 us
    pallas_call x1, Pallas kernels, whiten_sources(): pl.pallas_call(whiten_kernel, out_shape=jax.ShapeDtypeStruct((freqs, dept...  3.51 us
    broadcast_in_dim x2, local copies, waits for them, and re-layouts, gather_plane(): copies = jnp.broadcast_to(block, (16,) + block.shape)  2.85 us
  transfers between devices with their start and end apart: 9, of which 4 were waited for; matrix products, arithmetic and copies ran while one was open for 2% of the time, Pallas kernels for 4%

profile of v5, /device:TPU:1, one launch (start us, length us, event | category | flops | bytes accessed | tf_op | source)
XLA Modules:
  0.0 98.8 jit_solution(10392983482485313966)
XLA Ops:
  0.0 0.9 copy.2
  0.9 1.4 %broadcast_in_dim.6 = bf16[16,2,48,640]{3,2,1,0:T(8,128)(2,1)} broadcast(bf16[2,48,640]{2,1,0:T(8,128)(2,1)S(1)} %bitcast.11), dimensions={1,2,3} | broadcast | bytes 2088960 | tf_op jit(solution)/shard_map/broadcast_in_dim | solution.py:38
  2.3 7.6 %all-to-all-start = ((bf16[16,2,48,640]{3,2,1,0:T(8,128)(2,1)}), bf16[16,2,48,640]{3,2,1,0:T(8,128)(2,1)S(1)}, u32[]{:S(2)}, u32[]{:S(2)}) async-start(bf16[16,2,48,640]{3,2,1,0:T(8,128)(2,1)} %broadcast_in_dim.6), calls=%async_computation | async-start | bytes 3932160 | tf_op jit(solution)/shard_map/all_to_all | solution.py:39
  9.9 15.4 %collective-permute-start = (bf16[2,48,640]{2,1,0:T(8,128)(2,1)S(1)}, bf16[2,48,640]{2,1,0:T(8,128)(2,1)S(1)}, u32[]{:S(2)}, u32[]{:S(2)}) collective-permute-start(bf16[2,48,640]{2,1,0:T(8,128)(2,1)S(1)} %bitcast.12), channel_id=1, source_target_pairs={{0,1},{1,0},{2,3},{3,2},{4,5},{5,4},{6,7},{7,6},{8,9},{9,8},{10,11... | collective-permute-start | bytes 368648 | tf_op jit(solution)/shard_map/ppermute | solution.py:34
  25.4 0.1 fusion
  25.5 2.6 %collective-permute-done = bf16[2,48,640]{2,1,0:T(8,128)(2,1)S(1)} collective-permute-done((bf16[2,48,640]{2,1,0:T(8,128)(2,1)S(1)}, bf16[2,48,640]{2,1,0:T(8,128)(2,1)S(1)}, u32[]{:S(2)}, u32[]{:S(2)}) %collective-permute-start) | collective-permute-done | bytes 122912 | tf_op jit(solution)/shard_map/ppermute | solution.py:34
  28.1 0.1 fusion.1
  28.2 0.1 maximum_select_fusion
  28.4 10.4 %collective-permute-start.2 = (bf16[2,48,640]{2,1,0:T(8,128)(2,1)S(1)}, bf16[2,48,640]{2,1,0:T(8,128)(2,1)S(1)}, u32[]{:S(2)}, u32[]{:S(2)}) collective-permute-start(bf16[2,48,640]{2,1,0:T(8,128)(2,1)S(1)} %pad_maximum_fusion.1), channel_id=1, source_target_pairs={{0,256},{1,257},{2,0},{3,1},{4,288},{5,289},{6,32},{7,33},{8,320},... | collective-permute-start | bytes 368648 | tf_op jit(solution)/shard_map/ppermute | solution.py:34
  38.8 6.0 %collective-permute-start.1 = (bf16[2,48,640]{2,1,0:T(8,128)(2,1)S(1)}, bf16[2,48,640]{2,1,0:T(8,128)(2,1)S(1)}, u32[]{:S(2)}, u32[]{:S(2)}) collective-permute-start(bf16[2,48,640]{2,1,0:T(8,128)(2,1)S(1)} %pad_maximum_fusion.1), channel_id=1, source_target_pairs={{0,0},{1,1},{2,256},{3,257},{4,32},{5,33},{6,288},{7,289},{8,64},{... | collective-permute-start | bytes 368648 | tf_op jit(solution)/shard_map/ppermute | solution.py:34
  44.8 0.0 all-to-all-done.blocks.near
  44.8 1.4 %broadcast_in_dim.7 = bf16[16,2,48,640]{3,2,1,0:T(8,128)(2,1)} broadcast(bf16[2,48,640]{2,1,0:T(8,128)(2,1)S(1)} %collective-permute-done), dimensions={1,2,3} | broadcast | bytes 2088960 | tf_op jit(solution)/shard_map/broadcast_in_dim | solution.py:38
  46.2 11.1 %all-to-all-start.1 = ((bf16[16,2,48,640]{3,2,1,0:T(8,128)(2,1)}), bf16[16,2,48,640]{3,2,1,0:T(8,128)(2,1)}, u32[]{:S(2)}, u32[]{:S(2)}) async-start(bf16[16,2,48,640]{3,2,1,0:T(8,128)(2,1)} %broadcast_in_dim.7), calls=%async_computation.1 | async-start | bytes 3932160 | tf_op jit(solution)/shard_map/all_to_all | solution.py:39
  57.3 0.0 collective-permute-done.2
  57.3 0.0 collective-permute-done.1
  57.4 2.5 %collective-permute-start.5 = (bf16[2,2,48,640]{3,2,1,0:T(8,128)(2,1)S(1)}, bf16[2,2,48,640]{3,2,1,0:T(8,128)(2,1)S(1)}, u32[]{:S(2)}, u32[]{:S(2)}) collective-permute-start(bf16[2,2,48,640]{3,2,1,0:T(8,128)(2,1)S(1)} %pad_maximum_fusion), channel_id=1, source_target_pairs={{0,192},{1,193},{2,194},{3,195},{4,196},{5,197},{6,198},{7,199},{8... | collective-permute-start | bytes 737288 | tf_op jit(solution)/shard_map/ppermute | solution.py:34
  59.9 3.7 %collective-permute-start.4 = (bf16[2,2,48,640]{3,2,1,0:T(8,128)(2,1)S(1)}, bf16[2,2,48,640]{3,2,1,0:T(8,128)(2,1)S(1)}, u32[]{:S(2)}, u32[]{:S(2)}) collective-permute-start(bf16[2,2,48,640]{3,2,1,0:T(8,128)(2,1)S(1)} %pad_maximum_fusion), channel_id=1, source_target_pairs={{0,128},{1,129},{2,130},{3,131},{4,132},{5,133},{6,134},{7,135},{8... | collective-permute-start | bytes 737288 | tf_op jit(solution)/shard_map/ppermute | solution.py:34
  63.6 3.1 %collective-permute-start.3 = (bf16[2,2,48,640]{3,2,1,0:T(8,128)(2,1)S(1)}, bf16[2,2,48,640]{3,2,1,0:T(8,128)(2,1)S(1)}, u32[]{:S(2)}, u32[]{:S(2)}) collective-permute-start(bf16[2,2,48,640]{3,2,1,0:T(8,128)(2,1)S(1)} %pad_maximum_fusion), channel_id=1, source_target_pairs={{0,64},{1,65},{2,66},{3,67},{4,68},{5,69},{6,70},{7,71},{8,72},{9,... | collective-permute-start | bytes 737288 | tf_op jit(solution)/shard_map/ppermute | solution.py:34
  66.7 8.0 %collective-permute-done.3 = bf16[2,2,48,640]{3,2,1,0:T(8,128)(2,1)S(1)} collective-permute-done((bf16[2,2,48,640]{3,2,1,0:T(8,128)(2,1)S(1)}, bf16[2,2,48,640]{3,2,1,0:T(8,128)(2,1)S(1)}, u32[]{:S(2)}, u32[]{:S(2)}) %collective-permute-start.3) | collective-permute-done | bytes 245792 | tf_op jit(solution)/shard_map/ppermute | solution.py:34
  74.7 9.1 %collective-permute-done.4 = bf16[2,2,48,640]{3,2,1,0:T(8,128)(2,1)S(1)} collective-permute-done((bf16[2,2,48,640]{3,2,1,0:T(8,128)(2,1)S(1)}, bf16[2,2,48,640]{3,2,1,0:T(8,128)(2,1)S(1)}, u32[]{:S(2)}, u32[]{:S(2)}) %collective-permute-start.4) | collective-permute-done | bytes 245792 | tf_op jit(solution)/shard_map/ppermute | solution.py:34
  83.9 0.0 collective-permute-done.5
  83.9 2.3 %collective-permute-start.6 = (bf16[8,2,48,640]{3,2,1,0:T(8,128)(2,1)S(1)}, bf16[8,2,48,640]{3,2,1,0:T(8,128)(2,1)}, u32[]{:S(2)}, u32[]{:S(2)}) collective-permute-start(bf16[8,2,48,640]{3,2,1,0:T(8,128)(2,1)S(1)} %constant_dynamic-update-slice_fusion.held), channel_id=1, source_target_pairs={{0,32},{1,33},{2,34},{3,35},{4,36},{5,37},{6,38},{7,39},{8,40},{9,... | collective-permute-start | bytes 2949128 | tf_op jit(solution)/shard_map/ppermute | solution.py:34
  86.2 0.1 pad_add_fusion.place
  86.3 0.4 shard_map.17.energies
  86.7 2.0 %all-to-all-done.1.far = bf16[16,2,48,640]{3,2,1,0:T(8,128)(2,1)} async-done(((bf16[16,2,48,640]{3,2,1,0:T(8,128)(2,1)}), bf16[16,2,48,640]{3,2,1,0:T(8,128)(2,1)}, u32[]{:S(2)}, u32[]{:S(2)}) %all-to-all-start.1) | async-done | bytes 1966112 | tf_op jit(solution)/shard_map/all_to_all | solution.py:39
  88.7 3.5 %shard_map.18.wide = bf16[2,1536,1280]{2,1,0:T(8,128)(2,1)S(1)} custom-call(bf16[16,2,48,640]{3,2,1,0:T(8,128)(2,1)S(1)} %all-to-all-done.blocks.near, bf16[16,2,48,640]{3,2,1,0:T(8,128)(2,1)} %all-to-all-done.1.far, f32[2,8,640]{2,1,0:T(8,128)S(1)} %shard_map.17.energies), custom_call_target="tpu_custom_call" | custom-call | tf_op jit(solution)/shard_map/pallas_call | solution.py:175
  92.2 0.0 collective-permute-done.6.other
  92.2 6.5 %shard_map.19 = f32[2,2,320,640]{3,2,1,0:T(8,128)} custom-call(s32[4]{0:T(128)S(1)} %pad_add_fusion.place, bf16[8,2,48,640]{3,2,1,0:T(8,128)(2,1)S(1)} %constant_dynamic-update-slice_fusion.held, bf16[8,2,48,640]{3,2,1,0:T(8,128)(2,1)} %collective-permute-done.6.other, bf16[2,1536,1280]{2,1,0:T(8,128)(2,1)S(1)} %shard_map.18.wide), custom_call_target="tpu_custom_call" | custom-call | tf_op jit(solution)/shard_map/pallas_call | solution.py:187
  (7 shorter events, 0.2 us)
Async XLA Ops:
  2.3 42.4 %all-to-all-start = ((bf16[16,2,48,640]{3,2,1,0:T(8,128)(2,1)}), bf16[16,2,48,640]{3,2,1,0:T(8,128)(2,1)S(1)}, u32[]{:S(2)}, u32[]{:S(2)}) async-start(bf16[16,2,48,640]{3,2,1,0:T(8,128)(2,1)} %broadcast_in_dim.6), calls=%async_computation | async-start | bytes 3932160 | tf_op jit(solution)/shard_map/all_to_all | solution.py:39
  9.9 18.2 %collective-permute-start = (bf16[2,48,640]{2,1,0:T(8,128)(2,1)S(1)}, bf16[2,48,640]{2,1,0:T(8,128)(2,1)S(1)}, u32[]{:S(2)}, u32[]{:S(2)}) collective-permute-start(bf16[2,48,640]{2,1,0:T(8,128)(2,1)S(1)} %bitcast.12), channel_id=1, source_target_pairs={{0,1},{1,0},{2,3},{3,2},{4,5},{5,4},{6,7},{7,6},{8,9},{9,8},{10,11... | collective-permute-start | bytes 368648 | tf_op jit(solution)/shard_map/ppermute | solution.py:34
  28.4 28.9 %collective-permute-start.2 = (bf16[2,48,640]{2,1,0:T(8,128)(2,1)S(1)}, bf16[2,48,640]{2,1,0:T(8,128)(2,1)S(1)}, u32[]{:S(2)}, u32[]{:S(2)}) collective-permute-start(bf16[2,48,640]{2,1,0:T(8,128)(2,1)S(1)} %pad_maximum_fusion.1), channel_id=1, source_target_pairs={{0,256},{1,257},{2,0},{3,1},{4,288},{5,289},{6,32},{7,33},{8,320},... | collective-permute-start | bytes 368648 | tf_op jit(solution)/shard_map/ppermute | solution.py:34
  38.8 18.5 %collective-permute-start.1 = (bf16[2,48,640]{2,1,0:T(8,128)(2,1)S(1)}, bf16[2,48,640]{2,1,0:T(8,128)(2,1)S(1)}, u32[]{:S(2)}, u32[]{:S(2)}) collective-permute-start(bf16[2,48,640]{2,1,0:T(8,128)(2,1)S(1)} %pad_maximum_fusion.1), channel_id=1, source_target_pairs={{0,0},{1,1},{2,256},{3,257},{4,32},{5,33},{6,288},{7,289},{8,64},{... | collective-permute-start | bytes 368648 | tf_op jit(solution)/shard_map/ppermute | solution.py:34
  46.2 42.5 %all-to-all-start.1 = ((bf16[16,2,48,640]{3,2,1,0:T(8,128)(2,1)}), bf16[16,2,48,640]{3,2,1,0:T(8,128)(2,1)}, u32[]{:S(2)}, u32[]{:S(2)}) async-start(bf16[16,2,48,640]{3,2,1,0:T(8,128)(2,1)} %broadcast_in_dim.7), calls=%async_computation.1 | async-start | bytes 3932160 | tf_op jit(solution)/shard_map/all_to_all | solution.py:39
  57.4 26.5 %collective-permute-start.5 = (bf16[2,2,48,640]{3,2,1,0:T(8,128)(2,1)S(1)}, bf16[2,2,48,640]{3,2,1,0:T(8,128)(2,1)S(1)}, u32[]{:S(2)}, u32[]{:S(2)}) collective-permute-start(bf16[2,2,48,640]{3,2,1,0:T(8,128)(2,1)S(1)} %pad_maximum_fusion), channel_id=1, source_target_pairs={{0,192},{1,193},{2,194},{3,195},{4,196},{5,197},{6,198},{7,199},{8... | collective-permute-start | bytes 737288 | tf_op jit(solution)/shard_map/ppermute | solution.py:34
  59.9 24.0 %collective-permute-start.4 = (bf16[2,2,48,640]{3,2,1,0:T(8,128)(2,1)S(1)}, bf16[2,2,48,640]{3,2,1,0:T(8,128)(2,1)S(1)}, u32[]{:S(2)}, u32[]{:S(2)}) collective-permute-start(bf16[2,2,48,640]{3,2,1,0:T(8,128)(2,1)S(1)} %pad_maximum_fusion), channel_id=1, source_target_pairs={{0,128},{1,129},{2,130},{3,131},{4,132},{5,133},{6,134},{7,135},{8... | collective-permute-start | bytes 737288 | tf_op jit(solution)/shard_map/ppermute | solution.py:34
  63.6 11.1 %collective-permute-start.3 = (bf16[2,2,48,640]{3,2,1,0:T(8,128)(2,1)S(1)}, bf16[2,2,48,640]{3,2,1,0:T(8,128)(2,1)S(1)}, u32[]{:S(2)}, u32[]{:S(2)}) collective-permute-start(bf16[2,2,48,640]{3,2,1,0:T(8,128)(2,1)S(1)} %pad_maximum_fusion), channel_id=1, source_target_pairs={{0,64},{1,65},{2,66},{3,67},{4,68},{5,69},{6,70},{7,71},{8,72},{9,... | collective-permute-start | bytes 737288 | tf_op jit(solution)/shard_map/ppermute | solution.py:34
  83.9 8.3 %collective-permute-start.6 = (bf16[8,2,48,640]{3,2,1,0:T(8,128)(2,1)S(1)}, bf16[8,2,48,640]{3,2,1,0:T(8,128)(2,1)}, u32[]{:S(2)}, u32[]{:S(2)}) collective-permute-start(bf16[8,2,48,640]{3,2,1,0:T(8,128)(2,1)S(1)} %constant_dynamic-update-slice_fusion.held), channel_id=1, source_target_pairs={{0,32},{1,33},{2,34},{3,35},{4,36},{5,37},{6,38},{7,39},{8,40},{9,... | collective-permute-start | bytes 2949128 | tf_op jit(solution)/shard_map/ppermute | solution.py:34

commit v6 on v5

--- a/solution.py
+++ b/solution.py
@@ -83,18 +83,23 @@
         out[f] = lax.fori_loop(0, 4, add, jnp.zeros((8, channels), jnp.float32))
 
 
-def whiten_kernel(near, far, energies, wide):
+def whiten_kernel(near, arrived, energies, wide, far, sems):
     sources = (near, far)
     freqs, rows, channels = sources[0].shape[1:]
     windows = 16 * rows
+    copies = [
+        pltpu.make_async_copy(arrived.at[pl.ds(4 * n, 4)], far.at[pl.ds(4 * n, 4)], sems.at[n]) for n in range(4)
+    ]
+    for copy in copies:
+        copy.start()
+    totals = [energies[f] for f in range(freqs)]
+    for n, copy in enumerate(copies):
+        copy.wait()
+        for f in range(freqs):
+            for i in range(4):
+                totals[f] = totals[f] + fold(energy_of(far[4 * n + i, f])[2])
     for f in range(freqs):
-
-        def add(a, total):
-            for i in range(4):
-                total = total + fold(energy_of(far[a * 4 + i, f])[2])
-            return total
-
-        floor = floor_of(lax.fori_loop(0, 4, add, energies[f]), windows)
+        floor = floor_of(totals[f], windows)
 
         def whiten(a, carry):
             for i in range(4):
@@ -110,19 +115,26 @@
         lax.fori_loop(0, 4, whiten, 0)
 
 
-def multiply_kernel(place, held, other, wide, out, left, products, sems):
+def multiply_kernel(place, held, arrived, wide, out, other, left, products, sems, other_sem):
     zl, core, column = place[0], place[1], place[2] * 4 + place[3]
     rows, channels = held.shape[2:]
     width = channels // 2
     windows = 16 * rows
 
-    def add(a, total):
-        for ref in (held, other):
+    fetch = pltpu.make_async_copy(arrived, other, other_sem)
+    fetch.start()
+
+    def energies_in(ref, total):
+        def add(a, total):
             for zr in range(2):
                 total = total + fold(energy_of(ref[a, zr])[2])
-        return total
-
-    floor = floor_of(lax.fori_loop(0, 8, add, jnp.zeros((8, channels), jnp.float32)), windows)
+            return total
+
+        return lax.fori_loop(0, 8, add, total)
+
+    total = energies_in(held, jnp.zeros((8, channels), jnp.float32))
+    fetch.wait()
+    floor = floor_of(energies_in(other, total), windows)
 
     def whiten(a, carry):
         along = lax.rem(lax.bitwise_xor(zl, a // 2), 4)
@@ -175,8 +187,9 @@
     return pl.pallas_call(
         whiten_kernel,
         out_shape=jax.ShapeDtypeStruct((freqs, depth, 2 * channels), jnp.bfloat16),
-        in_specs=[VMEM] * 3,
+        in_specs=[VMEM, pl.BlockSpec(memory_space=pl.ANY), VMEM],
         out_specs=VMEM,
+        scratch_shapes=[pltpu.VMEM(far.shape, far.dtype), pltpu.SemaphoreType.DMA((4,))],
         compiler_params=pltpu.CompilerParams(vmem_limit_bytes=20 * 1024 * 1024),
     )(near, far, energies)
 
@@ -187,12 +200,14 @@
     return pl.pallas_call(
         multiply_kernel,
         out_shape=jax.ShapeDtypeStruct((2, 2, width, channels), jnp.float32),
-        in_specs=[SMEM, VMEM, VMEM, VMEM],
+        in_specs=[SMEM, VMEM, pl.BlockSpec(memory_space=pl.ANY), VMEM],
         out_specs=pl.BlockSpec(memory_space=pl.ANY),
         scratch_shapes=[
+            pltpu.VMEM(other.shape, other.dtype),
             pltpu.VMEM((2, depth, width), jnp.bfloat16),
             pltpu.VMEM((2, 2, width, channels), jnp.float32),
             pltpu.SemaphoreType.DMA((2, 2)),
+            pltpu.SemaphoreType.DMA,
         ],
         compiler_params=pltpu.CompilerParams(vmem_limit_bytes=20 * 1024 * 1024),
     )(place, held, other, wide)

time: 99.2 us -> 99.2 us (level)
  no operation moved by 1% of the time
where the time goes in v6:
time: 99.2 us; the launch traced here: 98.8 us
  starting transfers between devices  62.1 us (63%)
  waiting for transfers between devices  21.7 us (22%)
  Pallas kernels  10.5 us (11%)
  local copies, waits for them, and re-layouts  4.07 us (4%)
    ppermute x7, starting transfers between devices, permute(): return lax.ppermute(value, AXES, pairs)  43.4 us
    ppermute x7, waiting for transfers between devices, permute(): return lax.ppermute(value, AXES, pairs)  19.7 us
    all_to_all x2, starting transfers between devices, gather_plane(): return lax.all_to_all(copies, ('y', 'x'), 0, 0)  18.6 us
    pallas_call x1, Pallas kernels, multiply(): pl.pallas_call(multiply_kernel, out_shape=jax.ShapeDtypeStruct((2, 2, wid...  6.9 us
    pallas_call x1, Pallas kernels, whiten_sources(): pl.pallas_call(whiten_kernel, out_shape=jax.ShapeDtypeStruct((freqs, dept...  3.15 us
    broadcast_in_dim x2, local copies, waits for them, and re-layouts, gather_plane(): copies = jnp.broadcast_to(block, (16,) + block.shape)  2.85 us
  transfers between devices with their start and end apart: 9, of which 4 were waited for; matrix products, arithmetic and copies ran while one was open for 2% of the time, Pallas kernels for 4%

profile of v6, /device:TPU:1, one launch (start us, length us, event | category | flops | bytes accessed | tf_op | source)
XLA Modules:
  0.0 98.8 jit_solution(5277912733907138613)
XLA Ops:
  0.0 0.9 copy.2
  0.9 1.4 %broadcast_in_dim.6 = bf16[16,2,48,640]{3,2,1,0:T(8,128)(2,1)} broadcast(bf16[2,48,640]{2,1,0:T(8,128)(2,1)S(1)} %bitcast.11), dimensions={1,2,3} | broadcast | bytes 2088960 | tf_op jit(solution)/shard_map/broadcast_in_dim | solution.py:38
  2.3 7.6 %all-to-all-start = ((bf16[16,2,48,640]{3,2,1,0:T(8,128)(2,1)}), bf16[16,2,48,640]{3,2,1,0:T(8,128)(2,1)S(1)}, u32[]{:S(2)}, u32[]{:S(2)}) async-start(bf16[16,2,48,640]{3,2,1,0:T(8,128)(2,1)} %broadcast_in_dim.6), calls=%async_computation | async-start | bytes 3932160 | tf_op jit(solution)/shard_map/all_to_all | solution.py:39
  9.9 15.4 %collective-permute-start = (bf16[2,48,640]{2,1,0:T(8,128)(2,1)S(1)}, bf16[2,48,640]{2,1,0:T(8,128)(2,1)S(1)}, u32[]{:S(2)}, u32[]{:S(2)}) collective-permute-start(bf16[2,48,640]{2,1,0:T(8,128)(2,1)S(1)} %bitcast.12), channel_id=1, source_target_pairs={{0,1},{1,0},{2,3},{3,2},{4,5},{5,4},{6,7},{7,6},{8,9},{9,8},{10,11... | collective-permute-start | bytes 368648 | tf_op jit(solution)/shard_map/ppermute | solution.py:34
  25.4 0.1 fusion
  25.5 2.6 %collective-permute-done = bf16[2,48,640]{2,1,0:T(8,128)(2,1)S(1)} collective-permute-done((bf16[2,48,640]{2,1,0:T(8,128)(2,1)S(1)}, bf16[2,48,640]{2,1,0:T(8,128)(2,1)S(1)}, u32[]{:S(2)}, u32[]{:S(2)}) %collective-permute-start) | collective-permute-done | bytes 122912 | tf_op jit(solution)/shard_map/ppermute | solution.py:34
  28.1 0.1 fusion.1
  28.2 0.1 maximum_select_fusion
  28.4 10.4 %collective-permute-start.2 = (bf16[2,48,640]{2,1,0:T(8,128)(2,1)S(1)}, bf16[2,48,640]{2,1,0:T(8,128)(2,1)S(1)}, u32[]{:S(2)}, u32[]{:S(2)}) collective-permute-start(bf16[2,48,640]{2,1,0:T(8,128)(2,1)S(1)} %pad_maximum_fusion.1), channel_id=1, source_target_pairs={{0,256},{1,257},{2,0},{3,1},{4,288},{5,289},{6,32},{7,33},{8,320},... | collective-permute-start | bytes 368648 | tf_op jit(solution)/shard_map/ppermute | solution.py:34
  38.8 6.0 %collective-permute-start.1 = (bf16[2,48,640]{2,1,0:T(8,128)(2,1)S(1)}, bf16[2,48,640]{2,1,0:T(8,128)(2,1)S(1)}, u32[]{:S(2)}, u32[]{:S(2)}) collective-permute-start(bf16[2,48,640]{2,1,0:T(8,128)(2,1)S(1)} %pad_maximum_fusion.1), channel_id=1, source_target_pairs={{0,0},{1,1},{2,256},{3,257},{4,32},{5,33},{6,288},{7,289},{8,64},{... | collective-permute-start | bytes 368648 | tf_op jit(solution)/shard_map/ppermute | solution.py:34
  44.8 0.0 all-to-all-done.blocks.near
  44.8 1.4 %broadcast_in_dim.7 = bf16[16,2,48,640]{3,2,1,0:T(8,128)(2,1)} broadcast(bf16[2,48,640]{2,1,0:T(8,128)(2,1)S(1)} %collective-permute-done), dimensions={1,2,3} | broadcast | bytes 2088960 | tf_op jit(solution)/shard_map/broadcast_in_dim | solution.py:38
  46.2 11.1 %all-to-all-start.1 = ((bf16[16,2,48,640]{3,2,1,0:T(8,128)(2,1)}), bf16[16,2,48,640]{3,2,1,0:T(8,128)(2,1)}, u32[]{:S(2)}, u32[]{:S(2)}) async-start(bf16[16,2,48,640]{3,2,1,0:T(8,128)(2,1)} %broadcast_in_dim.7), calls=%async_computation.1 | async-start | bytes 3932160 | tf_op jit(solution)/shard_map/all_to_all | solution.py:39
  57.3 0.0 collective-permute-done.2
  57.3 0.0 collective-permute-done.1
  57.4 2.5 %collective-permute-start.5 = (bf16[2,2,48,640]{3,2,1,0:T(8,128)(2,1)S(1)}, bf16[2,2,48,640]{3,2,1,0:T(8,128)(2,1)S(1)}, u32[]{:S(2)}, u32[]{:S(2)}) collective-permute-start(bf16[2,2,48,640]{3,2,1,0:T(8,128)(2,1)S(1)} %pad_maximum_fusion), channel_id=1, source_target_pairs={{0,192},{1,193},{2,194},{3,195},{4,196},{5,197},{6,198},{7,199},{8... | collective-permute-start | bytes 737288 | tf_op jit(solution)/shard_map/ppermute | solution.py:34
  59.9 3.7 %collective-permute-start.4 = (bf16[2,2,48,640]{3,2,1,0:T(8,128)(2,1)S(1)}, bf16[2,2,48,640]{3,2,1,0:T(8,128)(2,1)S(1)}, u32[]{:S(2)}, u32[]{:S(2)}) collective-permute-start(bf16[2,2,48,640]{3,2,1,0:T(8,128)(2,1)S(1)} %pad_maximum_fusion), channel_id=1, source_target_pairs={{0,128},{1,129},{2,130},{3,131},{4,132},{5,133},{6,134},{7,135},{8... | collective-permute-start | bytes 737288 | tf_op jit(solution)/shard_map/ppermute | solution.py:34
  63.6 3.1 %collective-permute-start.3 = (bf16[2,2,48,640]{3,2,1,0:T(8,128)(2,1)S(1)}, bf16[2,2,48,640]{3,2,1,0:T(8,128)(2,1)S(1)}, u32[]{:S(2)}, u32[]{:S(2)}) collective-permute-start(bf16[2,2,48,640]{3,2,1,0:T(8,128)(2,1)S(1)} %pad_maximum_fusion), channel_id=1, source_target_pairs={{0,64},{1,65},{2,66},{3,67},{4,68},{5,69},{6,70},{7,71},{8,72},{9,... | collective-permute-start | bytes 737288 | tf_op jit(solution)/shard_map/ppermute | solution.py:34
  66.7 8.0 %collective-permute-done.3 = bf16[2,2,48,640]{3,2,1,0:T(8,128)(2,1)S(1)} collective-permute-done((bf16[2,2,48,640]{3,2,1,0:T(8,128)(2,1)S(1)}, bf16[2,2,48,640]{3,2,1,0:T(8,128)(2,1)S(1)}, u32[]{:S(2)}, u32[]{:S(2)}) %collective-permute-start.3) | collective-permute-done | bytes 245792 | tf_op jit(solution)/shard_map/ppermute | solution.py:34
  74.7 9.1 %collective-permute-done.4 = bf16[2,2,48,640]{3,2,1,0:T(8,128)(2,1)S(1)} collective-permute-done((bf16[2,2,48,640]{3,2,1,0:T(8,128)(2,1)S(1)}, bf16[2,2,48,640]{3,2,1,0:T(8,128)(2,1)S(1)}, u32[]{:S(2)}, u32[]{:S(2)}) %collective-permute-start.4) | collective-permute-done | bytes 245792 | tf_op jit(solution)/shard_map/ppermute | solution.py:34
  83.9 0.0 collective-permute-done.5
  83.9 2.3 %collective-permute-start.6 = (bf16[8,2,48,640]{3,2,1,0:T(8,128)(2,1)S(1)}, bf16[8,2,48,640]{3,2,1,0:T(8,128)(2,1)}, u32[]{:S(2)}, u32[]{:S(2)}) collective-permute-start(bf16[8,2,48,640]{3,2,1,0:T(8,128)(2,1)S(1)} %constant_dynamic-update-slice_fusion.held), channel_id=1, source_target_pairs={{0,32},{1,33},{2,34},{3,35},{4,36},{5,37},{6,38},{7,39},{8,40},{9,... | collective-permute-start | bytes 2949128 | tf_op jit(solution)/shard_map/ppermute | solution.py:34
  86.2 0.1 pad_add_fusion.place
  86.3 0.4 shard_map.17.energies
  86.7 2.0 %all-to-all-done.1.arrived = bf16[16,2,48,640]{3,2,1,0:T(8,128)(2,1)} async-done(((bf16[16,2,48,640]{3,2,1,0:T(8,128)(2,1)}), bf16[16,2,48,640]{3,2,1,0:T(8,128)(2,1)}, u32[]{:S(2)}, u32[]{:S(2)}) %all-to-all-start.1) | async-done | bytes 1966112 | tf_op jit(solution)/shard_map/all_to_all | solution.py:39
  88.7 3.1 %shard_map.18.wide = bf16[2,1536,1280]{2,1,0:T(8,128)(2,1)S(1)} custom-call(bf16[16,2,48,640]{3,2,1,0:T(8,128)(2,1)S(1)} %all-to-all-done.blocks.near, bf16[16,2,48,640]{3,2,1,0:T(8,128)(2,1)} %all-to-all-done.1.arrived, f32[2,8,640]{2,1,0:T(8,128)S(1)} %shard_map.17.energies), custom_call_target="tpu_custom_call" | custom-call | tf_op jit(solution)/shard_map/pallas_call | solution.py:187
  91.9 0.0 collective-permute-done.6.arrived
  91.9 6.9 %shard_map.19 = f32[2,2,320,640]{3,2,1,0:T(8,128)} custom-call(s32[4]{0:T(128)S(1)} %pad_add_fusion.place, bf16[8,2,48,640]{3,2,1,0:T(8,128)(2,1)S(1)} %constant_dynamic-update-slice_fusion.held, bf16[8,2,48,640]{3,2,1,0:T(8,128)(2,1)} %collective-permute-done.6.arrived, bf16[2,1536,1280]{2,1,0:T(8,128)(2,1)S(1)} %shard_map.18.wide), custom_call_target="tpu_custom_call" | custom-call | tf_op jit(solution)/shard_map/pallas_call | solution.py:200
  (7 shorter events, 0.2 us)
Async XLA Ops:
  2.3 42.4 %all-to-all-start = ((bf16[16,2,48,640]{3,2,1,0:T(8,128)(2,1)}), bf16[16,2,48,640]{3,2,1,0:T(8,128)(2,1)S(1)}, u32[]{:S(2)}, u32[]{:S(2)}) async-start(bf16[16,2,48,640]{3,2,1,0:T(8,128)(2,1)} %broadcast_in_dim.6), calls=%async_computation | async-start | bytes 3932160 | tf_op jit(solution)/shard_map/all_to_all | solution.py:39
  9.9 18.2 %collective-permute-start = (bf16[2,48,640]{2,1,0:T(8,128)(2,1)S(1)}, bf16[2,48,640]{2,1,0:T(8,128)(2,1)S(1)}, u32[]{:S(2)}, u32[]{:S(2)}) collective-permute-start(bf16[2,48,640]{2,1,0:T(8,128)(2,1)S(1)} %bitcast.12), channel_id=1, source_target_pairs={{0,1},{1,0},{2,3},{3,2},{4,5},{5,4},{6,7},{7,6},{8,9},{9,8},{10,11... | collective-permute-start | bytes 368648 | tf_op jit(solution)/shard_map/ppermute | solution.py:34
  28.4 28.9 %collective-permute-start.2 = (bf16[2,48,640]{2,1,0:T(8,128)(2,1)S(1)}, bf16[2,48,640]{2,1,0:T(8,128)(2,1)S(1)}, u32[]{:S(2)}, u32[]{:S(2)}) collective-permute-start(bf16[2,48,640]{2,1,0:T(8,128)(2,1)S(1)} %pad_maximum_fusion.1), channel_id=1, source_target_pairs={{0,256},{1,257},{2,0},{3,1},{4,288},{5,289},{6,32},{7,33},{8,320},... | collective-permute-start | bytes 368648 | tf_op jit(solution)/shard_map/ppermute | solution.py:34
  38.8 18.5 %collective-permute-start.1 = (bf16[2,48,640]{2,1,0:T(8,128)(2,1)S(1)}, bf16[2,48,640]{2,1,0:T(8,128)(2,1)S(1)}, u32[]{:S(2)}, u32[]{:S(2)}) collective-permute-start(bf16[2,48,640]{2,1,0:T(8,128)(2,1)S(1)} %pad_maximum_fusion.1), channel_id=1, source_target_pairs={{0,0},{1,1},{2,256},{3,257},{4,32},{5,33},{6,288},{7,289},{8,64},{... | collective-permute-start | bytes 368648 | tf_op jit(solution)/shard_map/ppermute | solution.py:34
  46.2 42.5 %all-to-all-start.1 = ((bf16[16,2,48,640]{3,2,1,0:T(8,128)(2,1)}), bf16[16,2,48,640]{3,2,1,0:T(8,128)(2,1)}, u32[]{:S(2)}, u32[]{:S(2)}) async-start(bf16[16,2,48,640]{3,2,1,0:T(8,128)(2,1)} %broadcast_in_dim.7), calls=%async_computation.1 | async-start | bytes 3932160 | tf_op jit(solution)/shard_map/all_to_all | solution.py:39
  57.4 26.5 %collective-permute-start.5 = (bf16[2,2,48,640]{3,2,1,0:T(8,128)(2,1)S(1)}, bf16[2,2,48,640]{3,2,1,0:T(8,128)(2,1)S(1)}, u32[]{:S(2)}, u32[]{:S(2)}) collective-permute-start(bf16[2,2,48,640]{3,2,1,0:T(8,128)(2,1)S(1)} %pad_maximum_fusion), channel_id=1, source_target_pairs={{0,192},{1,193},{2,194},{3,195},{4,196},{5,197},{6,198},{7,199},{8... | collective-permute-start | bytes 737288 | tf_op jit(solution)/shard_map/ppermute | solution.py:34
  59.9 24.0 %collective-permute-start.4 = (bf16[2,2,48,640]{3,2,1,0:T(8,128)(2,1)S(1)}, bf16[2,2,48,640]{3,2,1,0:T(8,128)(2,1)S(1)}, u32[]{:S(2)}, u32[]{:S(2)}) collective-permute-start(bf16[2,2,48,640]{3,2,1,0:T(8,128)(2,1)S(1)} %pad_maximum_fusion), channel_id=1, source_target_pairs={{0,128},{1,129},{2,130},{3,131},{4,132},{5,133},{6,134},{7,135},{8... | collective-permute-start | bytes 737288 | tf_op jit(solution)/shard_map/ppermute | solution.py:34
  63.6 11.1 %collective-permute-start.3 = (bf16[2,2,48,640]{3,2,1,0:T(8,128)(2,1)S(1)}, bf16[2,2,48,640]{3,2,1,0:T(8,128)(2,1)S(1)}, u32[]{:S(2)}, u32[]{:S(2)}) collective-permute-start(bf16[2,2,48,640]{3,2,1,0:T(8,128)(2,1)S(1)} %pad_maximum_fusion), channel_id=1, source_target_pairs={{0,64},{1,65},{2,66},{3,67},{4,68},{5,69},{6,70},{7,71},{8,72},{9,... | collective-permute-start | bytes 737288 | tf_op jit(solution)/shard_map/ppermute | solution.py:34
  83.9 7.9 %collective-permute-start.6 = (bf16[8,2,48,640]{3,2,1,0:T(8,128)(2,1)S(1)}, bf16[8,2,48,640]{3,2,1,0:T(8,128)(2,1)}, u32[]{:S(2)}, u32[]{:S(2)}) collective-permute-start(bf16[8,2,48,640]{3,2,1,0:T(8,128)(2,1)S(1)} %constant_dynamic-update-slice_fusion.held), channel_id=1, source_target_pairs={{0,32},{1,33},{2,34},{3,35},{4,36},{5,37},{6,38},{7,39},{8,40},{9,... | collective-permute-start | bytes 2949128 | tf_op jit(solution)/shard_map/ppermute | solution.py:34

commit v7 on v6

--- a/solution.py
+++ b/solution.py
@@ -115,26 +115,19 @@
         lax.fori_loop(0, 4, whiten, 0)
 
 
-def multiply_kernel(place, held, arrived, wide, out, other, left, products, sems, other_sem):
+def multiply_kernel(place, held, other, wide, out, left, products, sems):
     zl, core, column = place[0], place[1], place[2] * 4 + place[3]
     rows, channels = held.shape[2:]
     width = channels // 2
     windows = 16 * rows
 
-    fetch = pltpu.make_async_copy(arrived, other, other_sem)
-    fetch.start()
-
-    def energies_in(ref, total):
-        def add(a, total):
+    def add(a, total):
+        for ref in (held, other):
             for zr in range(2):
                 total = total + fold(energy_of(ref[a, zr])[2])
-            return total
-
-        return lax.fori_loop(0, 8, add, total)
-
-    total = energies_in(held, jnp.zeros((8, channels), jnp.float32))
-    fetch.wait()
-    floor = floor_of(energies_in(other, total), windows)
+        return total
+
+    floor = floor_of(lax.fori_loop(0, 8, add, jnp.zeros((8, channels), jnp.float32)), windows)
 
     def whiten(a, carry):
         along = lax.rem(lax.bitwise_xor(zl, a // 2), 4)
@@ -200,14 +193,12 @@
     return pl.pallas_call(
         multiply_kernel,
         out_shape=jax.ShapeDtypeStruct((2, 2, width, channels), jnp.float32),
-        in_specs=[SMEM, VMEM, pl.BlockSpec(memory_space=pl.ANY), VMEM],
+        in_specs=[SMEM, VMEM, VMEM, VMEM],
         out_specs=pl.BlockSpec(memory_space=pl.ANY),
         scratch_shapes=[
-            pltpu.VMEM(other.shape, other.dtype),
             pltpu.VMEM((2, depth, width), jnp.bfloat16),
             pltpu.VMEM((2, 2, width, channels), jnp.float32),
             pltpu.SemaphoreType.DMA((2, 2)),
-            pltpu.SemaphoreType.DMA,
         ],
         compiler_params=pltpu.CompilerParams(vmem_limit_bytes=20 * 1024 * 1024),
     )(place, held, other, wide)

time: 99.2 us -> 98.9 us (level)
  no operation moved by 1% of the time
where the time goes in v7:
time: 98.9 us; the launch traced here: 98.4 us
  starting transfers between devices  62.1 us (63%)
  waiting for transfers between devices  21.7 us (22%)
  Pallas kernels  10.1 us (10%)
  local copies, waits for them, and re-layouts  4.07 us (4%)
    ppermute x7, starting transfers between devices, permute(): return lax.ppermute(value, AXES, pairs)  43.4 us
    ppermute x7, waiting for transfers between devices, permute(): return lax.ppermute(value, AXES, pairs)  19.7 us
    all_to_all x2, starting transfers between devices, gather_plane(): return lax.all_to_all(copies, ('y', 'x'), 0, 0)  18.6 us
    pallas_call x1, Pallas kernels, multiply(): pl.pallas_call(multiply_kernel, out_shape=jax.ShapeDtypeStruct((2, 2, wid...  6.55 us
    pallas_call x1, Pallas kernels, whiten_sources(): pl.pallas_call(whiten_kernel, out_shape=jax.ShapeDtypeStruct((freqs, dept...  3.15 us
    broadcast_in_dim x2, local copies, waits for them, and re-layouts, gather_plane(): copies = jnp.broadcast_to(block, (16,) + block.shape)  2.85 us
  transfers between devices with their start and end apart: 9, of which 4 were waited for; matrix products, arithmetic and copies ran while one was open for 2% of the time, Pallas kernels for 4%

profile of v7, /device:TPU:1, one launch (start us, length us, event | category | flops | bytes accessed | tf_op | source)
XLA Modules:
  0.0 98.4 jit_solution(4289289124374911144)
XLA Ops:
  0.0 0.9 copy.2
  0.9 1.4 %broadcast_in_dim.6 = bf16[16,2,48,640]{3,2,1,0:T(8,128)(2,1)} broadcast(bf16[2,48,640]{2,1,0:T(8,128)(2,1)S(1)} %bitcast.11), dimensions={1,2,3} | broadcast | bytes 2088960 | tf_op jit(solution)/shard_map/broadcast_in_dim | solution.py:38
  2.3 7.6 %all-to-all-start = ((bf16[16,2,48,640]{3,2,1,0:T(8,128)(2,1)}), bf16[16,2,48,640]{3,2,1,0:T(8,128)(2,1)S(1)}, u32[]{:S(2)}, u32[]{:S(2)}) async-start(bf16[16,2,48,640]{3,2,1,0:T(8,128)(2,1)} %broadcast_in_dim.6), calls=%async_computation | async-start | bytes 3932160 | tf_op jit(solution)/shard_map/all_to_all | solution.py:39
  9.9 15.4 %collective-permute-start = (bf16[2,48,640]{2,1,0:T(8,128)(2,1)S(1)}, bf16[2,48,640]{2,1,0:T(8,128)(2,1)S(1)}, u32[]{:S(2)}, u32[]{:S(2)}) collective-permute-start(bf16[2,48,640]{2,1,0:T(8,128)(2,1)S(1)} %bitcast.12), channel_id=1, source_target_pairs={{0,1},{1,0},{2,3},{3,2},{4,5},{5,4},{6,7},{7,6},{8,9},{9,8},{10,11... | collective-permute-start | bytes 368648 | tf_op jit(solution)/shard_map/ppermute | solution.py:34
  25.4 0.1 fusion
  25.5 2.6 %collective-permute-done = bf16[2,48,640]{2,1,0:T(8,128)(2,1)S(1)} collective-permute-done((bf16[2,48,640]{2,1,0:T(8,128)(2,1)S(1)}, bf16[2,48,640]{2,1,0:T(8,128)(2,1)S(1)}, u32[]{:S(2)}, u32[]{:S(2)}) %collective-permute-start) | collective-permute-done | bytes 122912 | tf_op jit(solution)/shard_map/ppermute | solution.py:34
  28.1 0.1 fusion.1
  28.2 0.1 maximum_select_fusion
  28.4 10.4 %collective-permute-start.2 = (bf16[2,48,640]{2,1,0:T(8,128)(2,1)S(1)}, bf16[2,48,640]{2,1,0:T(8,128)(2,1)S(1)}, u32[]{:S(2)}, u32[]{:S(2)}) collective-permute-start(bf16[2,48,640]{2,1,0:T(8,128)(2,1)S(1)} %pad_maximum_fusion.1), channel_id=1, source_target_pairs={{0,256},{1,257},{2,0},{3,1},{4,288},{5,289},{6,32},{7,33},{8,320},... | collective-permute-start | bytes 368648 | tf_op jit(solution)/shard_map/ppermute | solution.py:34
  38.8 6.0 %collective-permute-start.1 = (bf16[2,48,640]{2,1,0:T(8,128)(2,1)S(1)}, bf16[2,48,640]{2,1,0:T(8,128)(2,1)S(1)}, u32[]{:S(2)}, u32[]{:S(2)}) collective-permute-start(bf16[2,48,640]{2,1,0:T(8,128)(2,1)S(1)} %pad_maximum_fusion.1), channel_id=1, source_target_pairs={{0,0},{1,1},{2,256},{3,257},{4,32},{5,33},{6,288},{7,289},{8,64},{... | collective-permute-start | bytes 368648 | tf_op jit(solution)/shard_map/ppermute | solution.py:34
  44.8 0.0 all-to-all-done.blocks.near
  44.8 1.4 %broadcast_in_dim.7 = bf16[16,2,48,640]{3,2,1,0:T(8,128)(2,1)} broadcast(bf16[2,48,640]{2,1,0:T(8,128)(2,1)S(1)} %collective-permute-done), dimensions={1,2,3} | broadcast | bytes 2088960 | tf_op jit(solution)/shard_map/broadcast_in_dim | solution.py:38
  46.2 11.1 %all-to-all-start.1 = ((bf16[16,2,48,640]{3,2,1,0:T(8,128)(2,1)}), bf16[16,2,48,640]{3,2,1,0:T(8,128)(2,1)}, u32[]{:S(2)}, u32[]{:S(2)}) async-start(bf16[16,2,48,640]{3,2,1,0:T(8,128)(2,1)} %broadcast_in_dim.7), calls=%async_computation.1 | async-start | bytes 3932160 | tf_op jit(solution)/shard_map/all_to_all | solution.py:39
  57.3 0.0 collective-permute-done.2
  57.3 0.0 collective-permute-done.1
  57.4 2.5 %collective-permute-start.5 = (bf16[2,2,48,640]{3,2,1,0:T(8,128)(2,1)S(1)}, bf16[2,2,48,640]{3,2,1,0:T(8,128)(2,1)S(1)}, u32[]{:S(2)}, u32[]{:S(2)}) collective-permute-start(bf16[2,2,48,640]{3,2,1,0:T(8,128)(2,1)S(1)} %pad_maximum_fusion), channel_id=1, source_target_pairs={{0,192},{1,193},{2,194},{3,195},{4,196},{5,197},{6,198},{7,199},{8... | collective-permute-start | bytes 737288 | tf_op jit(solution)/shard_map/ppermute | solution.py:34
  59.9 3.7 %collective-permute-start.4 = (bf16[2,2,48,640]{3,2,1,0:T(8,128)(2,1)S(1)}, bf16[2,2,48,640]{3,2,1,0:T(8,128)(2,1)S(1)}, u32[]{:S(2)}, u32[]{:S(2)}) collective-permute-start(bf16[2,2,48,640]{3,2,1,0:T(8,128)(2,1)S(1)} %pad_maximum_fusion), channel_id=1, source_target_pairs={{0,128},{1,129},{2,130},{3,131},{4,132},{5,133},{6,134},{7,135},{8... | collective-permute-start | bytes 737288 | tf_op jit(solution)/shard_map/ppermute | solution.py:34
  63.6 3.1 %collective-permute-start.3 = (bf16[2,2,48,640]{3,2,1,0:T(8,128)(2,1)S(1)}, bf16[2,2,48,640]{3,2,1,0:T(8,128)(2,1)S(1)}, u32[]{:S(2)}, u32[]{:S(2)}) collective-permute-start(bf16[2,2,48,640]{3,2,1,0:T(8,128)(2,1)S(1)} %pad_maximum_fusion), channel_id=1, source_target_pairs={{0,64},{1,65},{2,66},{3,67},{4,68},{5,69},{6,70},{7,71},{8,72},{9,... | collective-permute-start | bytes 737288 | tf_op jit(solution)/shard_map/ppermute | solution.py:34
  66.7 8.0 %collective-permute-done.3 = bf16[2,2,48,640]{3,2,1,0:T(8,128)(2,1)S(1)} collective-permute-done((bf16[2,2,48,640]{3,2,1,0:T(8,128)(2,1)S(1)}, bf16[2,2,48,640]{3,2,1,0:T(8,128)(2,1)S(1)}, u32[]{:S(2)}, u32[]{:S(2)}) %collective-permute-start.3) | collective-permute-done | bytes 245792 | tf_op jit(solution)/shard_map/ppermute | solution.py:34
  74.7 9.1 %collective-permute-done.4 = bf16[2,2,48,640]{3,2,1,0:T(8,128)(2,1)S(1)} collective-permute-done((bf16[2,2,48,640]{3,2,1,0:T(8,128)(2,1)S(1)}, bf16[2,2,48,640]{3,2,1,0:T(8,128)(2,1)S(1)}, u32[]{:S(2)}, u32[]{:S(2)}) %collective-permute-start.4) | collective-permute-done | bytes 245792 | tf_op jit(solution)/shard_map/ppermute | solution.py:34
  83.9 0.0 collective-permute-done.5
  83.9 2.3 %collective-permute-start.6 = (bf16[8,2,48,640]{3,2,1,0:T(8,128)(2,1)S(1)}, bf16[8,2,48,640]{3,2,1,0:T(8,128)(2,1)}, u32[]{:S(2)}, u32[]{:S(2)}) collective-permute-start(bf16[8,2,48,640]{3,2,1,0:T(8,128)(2,1)S(1)} %constant_dynamic-update-slice_fusion.held), channel_id=1, source_target_pairs={{0,32},{1,33},{2,34},{3,35},{4,36},{5,37},{6,38},{7,39},{8,40},{9,... | collective-permute-start | bytes 2949128 | tf_op jit(solution)/shard_map/ppermute | solution.py:34
  86.2 0.1 pad_add_fusion.place
  86.3 0.4 shard_map.17.energies
  86.7 2.0 %all-to-all-done.1.arrived = bf16[16,2,48,640]{3,2,1,0:T(8,128)(2,1)} async-done(((bf16[16,2,48,640]{3,2,1,0:T(8,128)(2,1)}), bf16[16,2,48,640]{3,2,1,0:T(8,128)(2,1)}, u32[]{:S(2)}, u32[]{:S(2)}) %all-to-all-start.1) | async-done | bytes 1966112 | tf_op jit(solution)/shard_map/all_to_all | solution.py:39
  88.7 3.1 %shard_map.18.wide = bf16[2,1536,1280]{2,1,0:T(8,128)(2,1)S(1)} custom-call(bf16[16,2,48,640]{3,2,1,0:T(8,128)(2,1)S(1)} %all-to-all-done.blocks.near, bf16[16,2,48,640]{3,2,1,0:T(8,128)(2,1)} %all-to-all-done.1.arrived, f32[2,8,640]{2,1,0:T(8,128)S(1)} %shard_map.17.energies), custom_call_target="tpu_custom_call" | custom-call | tf_op jit(solution)/shard_map/pallas_call | solution.py:180
  91.9 0.0 collective-permute-done.6.other
  91.9 6.5 %shard_map.19 = f32[2,2,320,640]{3,2,1,0:T(8,128)} custom-call(s32[4]{0:T(128)S(1)} %pad_add_fusion.place, bf16[8,2,48,640]{3,2,1,0:T(8,128)(2,1)S(1)} %constant_dynamic-update-slice_fusion.held, bf16[8,2,48,640]{3,2,1,0:T(8,128)(2,1)} %collective-permute-done.6.other, bf16[2,1536,1280]{2,1,0:T(8,128)(2,1)S(1)} %shard_map.18.wide), custom_call_target="tpu_custom_call" | custom-call | tf_op jit(solution)/shard_map/pallas_call | solution.py:193
  (7 shorter events, 0.2 us)
Async XLA Ops:
  2.3 42.4 %all-to-all-start = ((bf16[16,2,48,640]{3,2,1,0:T(8,128)(2,1)}), bf16[16,2,48,640]{3,2,1,0:T(8,128)(2,1)S(1)}, u32[]{:S(2)}, u32[]{:S(2)}) async-start(bf16[16,2,48,640]{3,2,1,0:T(8,128)(2,1)} %broadcast_in_dim.6), calls=%async_computation | async-start | bytes 3932160 | tf_op jit(solution)/shard_map/all_to_all | solution.py:39
  9.9 18.2 %collective-permute-start = (bf16[2,48,640]{2,1,0:T(8,128)(2,1)S(1)}, bf16[2,48,640]{2,1,0:T(8,128)(2,1)S(1)}, u32[]{:S(2)}, u32[]{:S(2)}) collective-permute-start(bf16[2,48,640]{2,1,0:T(8,128)(2,1)S(1)} %bitcast.12), channel_id=1, source_target_pairs={{0,1},{1,0},{2,3},{3,2},{4,5},{5,4},{6,7},{7,6},{8,9},{9,8},{10,11... | collective-permute-start | bytes 368648 | tf_op jit(solution)/shard_map/ppermute | solution.py:34
  28.4 28.9 %collective-permute-start.2 = (bf16[2,48,640]{2,1,0:T(8,128)(2,1)S(1)}, bf16[2,48,640]{2,1,0:T(8,128)(2,1)S(1)}, u32[]{:S(2)}, u32[]{:S(2)}) collective-permute-start(bf16[2,48,640]{2,1,0:T(8,128)(2,1)S(1)} %pad_maximum_fusion.1), channel_id=1, source_target_pairs={{0,256},{1,257},{2,0},{3,1},{4,288},{5,289},{6,32},{7,33},{8,320},... | collective-permute-start | bytes 368648 | tf_op jit(solution)/shard_map/ppermute | solution.py:34
  38.8 18.5 %collective-permute-start.1 = (bf16[2,48,640]{2,1,0:T(8,128)(2,1)S(1)}, bf16[2,48,640]{2,1,0:T(8,128)(2,1)S(1)}, u32[]{:S(2)}, u32[]{:S(2)}) collective-permute-start(bf16[2,48,640]{2,1,0:T(8,128)(2,1)S(1)} %pad_maximum_fusion.1), channel_id=1, source_target_pairs={{0,0},{1,1},{2,256},{3,257},{4,32},{5,33},{6,288},{7,289},{8,64},{... | collective-permute-start | bytes 368648 | tf_op jit(solution)/shard_map/ppermute | solution.py:34
  46.2 42.5 %all-to-all-start.1 = ((bf16[16,2,48,640]{3,2,1,0:T(8,128)(2,1)}), bf16[16,2,48,640]{3,2,1,0:T(8,128)(2,1)}, u32[]{:S(2)}, u32[]{:S(2)}) async-start(bf16[16,2,48,640]{3,2,1,0:T(8,128)(2,1)} %broadcast_in_dim.7), calls=%async_computation.1 | async-start | bytes 3932160 | tf_op jit(solution)/shard_map/all_to_all | solution.py:39
  57.4 26.5 %collective-permute-start.5 = (bf16[2,2,48,640]{3,2,1,0:T(8,128)(2,1)S(1)}, bf16[2,2,48,640]{3,2,1,0:T(8,128)(2,1)S(1)}, u32[]{:S(2)}, u32[]{:S(2)}) collective-permute-start(bf16[2,2,48,640]{3,2,1,0:T(8,128)(2,1)S(1)} %pad_maximum_fusion), channel_id=1, source_target_pairs={{0,192},{1,193},{2,194},{3,195},{4,196},{5,197},{6,198},{7,199},{8... | collective-permute-start | bytes 737288 | tf_op jit(solution)/shard_map/ppermute | solution.py:34
  59.9 24.0 %collective-permute-start.4 = (bf16[2,2,48,640]{3,2,1,0:T(8,128)(2,1)S(1)}, bf16[2,2,48,640]{3,2,1,0:T(8,128)(2,1)S(1)}, u32[]{:S(2)}, u32[]{:S(2)}) collective-permute-start(bf16[2,2,48,640]{3,2,1,0:T(8,128)(2,1)S(1)} %pad_maximum_fusion), channel_id=1, source_target_pairs={{0,128},{1,129},{2,130},{3,131},{4,132},{5,133},{6,134},{7,135},{8... | collective-permute-start | bytes 737288 | tf_op jit(solution)/shard_map/ppermute | solution.py:34
  63.6 11.1 %collective-permute-start.3 = (bf16[2,2,48,640]{3,2,1,0:T(8,128)(2,1)S(1)}, bf16[2,2,48,640]{3,2,1,0:T(8,128)(2,1)S(1)}, u32[]{:S(2)}, u32[]{:S(2)}) collective-permute-start(bf16[2,2,48,640]{3,2,1,0:T(8,128)(2,1)S(1)} %pad_maximum_fusion), channel_id=1, source_target_pairs={{0,64},{1,65},{2,66},{3,67},{4,68},{5,69},{6,70},{7,71},{8,72},{9,... | collective-permute-start | bytes 737288 | tf_op jit(solution)/shard_map/ppermute | solution.py:34
  83.9 7.9 %collective-permute-start.6 = (bf16[8,2,48,640]{3,2,1,0:T(8,128)(2,1)S(1)}, bf16[8,2,48,640]{3,2,1,0:T(8,128)(2,1)}, u32[]{:S(2)}, u32[]{:S(2)}) collective-permute-start(bf16[8,2,48,640]{3,2,1,0:T(8,128)(2,1)S(1)} %constant_dynamic-update-slice_fusion.held), channel_id=1, source_target_pairs={{0,32},{1,33},{2,34},{3,35},{4,36},{5,37},{6,38},{7,39},{8,40},{9,... | collective-permute-start | bytes 2949128 | tf_op jit(solution)/shard_map/ppermute | solution.py:34
